TPU v7x, 32 devices: a whole 2x2x4 slice. The times are simulated.
32 devices in a mesh: group: 2 (over y), seq: 4 (over z), fsdp: 4 (over x, core).
Axes of the slice: x: 2, y: 2, z: 4, core: 2. Of those that a mesh axis runs over, the one named last changes fastest.
Arguments:
- tile_patches: bfloat16 [64, 256, 1536], P(('group', 'seq', 'fsdp')), parts along dimension 0, may hold values from -6 to 6
- vit_gain: float32 [1536], replicated, may hold values from 0.25 to 1.75
- w_query: bfloat16 [1536, 768], P('fsdp'), may hold values from -0.15625 to 0.15625
- w_key: bfloat16 [1536, 768], P('fsdp'), may hold values from -0.15625 to 0.15625
- w_value: bfloat16 [1536, 768], P('fsdp'), may hold values from -0.15625 to 0.15625
- w_out: bfloat16 [768, 1536], P('fsdp'), may hold values from -0.21875 to 0.21875
- w_proj: bfloat16 [1536, 768], P('fsdp'), may hold values from -0.15625 to 0.15625
- long_gain: float32 [768], replicated, may hold values from 0.25 to 1.75
- long_query: bfloat16 [768, 768], P(None, 'fsdp'), may hold values from -0.21875 to 0.21875
- long_key: bfloat16 [768, 768], P(None, 'fsdp'), may hold values from -0.21875 to 0.21875
- long_value: bfloat16 [768, 768], P(None, 'fsdp'), may hold values from -0.21875 to 0.21875
- long_out: bfloat16 [768, 768], P('fsdp'), may hold values from -0.21875 to 0.21875
- seq_order: int32 [64], P(('group', 'seq', 'fsdp')), parts along dimension 0, may hold values from 0 to 31, each once
- counts: int32 [32], P(('group', 'seq', 'fsdp')), parts along dimension 0, may hold values from 1 to 2
Outputs:
- encoded: bfloat16 [64, 768], P(('group', 'seq'), 'fsdp'), parts along dimension 0
There are 2 independent parts, one for each index of `group`. A program takes and returns all parts, laid end to end along the dimension named above; an argument that names none is the same for every part. Nothing has to cross between parts.
Inputs may be any that keep to these rules, and one draw needn't show every extreme that they name: `seq_order`: each of the 32 sequence positions belongs to exactly one tile. In each block of 2 consecutive tiles the first counts tiles are tissue.
All inputs are finite; a program needn't handle non-finite values.
Results may differ from a plain program's by a relative error of at most 0.013.
Values may be sent and summed in bfloat16 or wider, within the bound.
A program may use at most 64 MiB of HBM per device.

v0:
```python
import math

import jax
import jax.numpy as jnp
from jax import lax
from jax.sharding import PartitionSpec as P

VHD = 64
HEADS = 16
DILATION_STEP = 4


EPSILON = 1e-06


def layer_norm(inputs, norm_gain):
    widened = inputs.astype(jnp.float32)
    average = jnp.mean(widened, axis=-1, keepdims=True)
    centred = widened - average
    variance = jnp.mean(centred * centred, axis=-1, keepdims=True)
    return (centred * lax.rsqrt(variance + EPSILON) * norm_gain).astype(jnp.bfloat16)


def dilated_attention(
    query_rows,
    key_rows,
    value_rows,
    query_position_index,
    key_position_index,
    key_present,
    leading_head,
    head_total_count,
    segment,
):
    head_size = query_rows.shape[1] // head_total_count
    query_heads = query_rows.reshape(query_rows.shape[0], head_total_count, head_size)
    key_heads = key_rows.reshape(key_rows.shape[0], head_total_count, head_size)
    value_heads = value_rows.reshape(value_rows.shape[0], head_total_count, head_size)
    scores = jnp.einsum(
        "rhd,khd->hrk", query_heads, key_heads, preferred_element_type=jnp.float32
    ) / math.sqrt(head_size)
    itself = query_position_index[:, None] == key_position_index[None, :]
    permitted_mask = (key_present[None, :] > 0) | itself
    in_local = (
        query_position_index[:, None] // segment == key_position_index[None, :] // segment
    ) & permitted_mask
    head_shift_amounts = (
        leading_head + jnp.arange(head_total_count, dtype=jnp.int32)
    ) % DILATION_STEP
    within_dilated_set = (
        ((query_position_index % DILATION_STEP)[None, :, None] == head_shift_amounts[:, None, None])
        & ((key_position_index % DILATION_STEP)[None, None, :] == head_shift_amounts[:, None, None])
        & permitted_mask[None]
    )
    lifted = jnp.exp(scores)
    local_weights = jnp.where(in_local[None], lifted, 0.0)
    dilated_weights = jnp.where(within_dilated_set, lifted, 0.0)
    denominator = jnp.sum(local_weights, axis=-1) + jnp.sum(dilated_weights, axis=-1)
    numerator = jnp.einsum(
        "hrk,khd->rhd",
        local_weights.astype(jnp.bfloat16),
        value_heads,
        preferred_element_type=jnp.float32,
    )
    numerator = numerator + jnp.einsum(
        "hrk,khd->rhd",
        dilated_weights.astype(jnp.bfloat16),
        value_heads,
        preferred_element_type=jnp.float32,
    )
    combined = numerator / jnp.transpose(denominator)[:, :, None]
    return combined.reshape(query_rows.shape[0], head_total_count * head_size).astype(jnp.bfloat16)


def local(
    tile_patches,
    vit_gain,
    w_query,
    w_key,
    w_value,
    w_out,
    w_proj,
    long_gain,
    long_query,
    long_key,
    long_value,
    long_out,
    seq_order,
    counts,
):
    seq_size = lax.axis_size("seq")
    group_size = lax.axis_size("fsdp")
    tile_count, patch_count, width = tile_patches.shape
    normed = layer_norm(tile_patches, vit_gain)
    class_normed = normed[:, 0, :]
    vit_width = w_key.shape[1]
    vit_heads = vit_width // VHD
    full_query, full_out, full_proj = (
        lax.all_gather(w_query, "fsdp", axis=0, tiled=True),
        lax.all_gather(w_out, "fsdp", axis=0, tiled=True),
        lax.all_gather(w_proj, "fsdp", axis=0, tiled=True),
    )
    query_row = jnp.dot(class_normed, full_query, preferred_element_type=jnp.float32).astype(
        jnp.bfloat16
    )
    group_query = lax.all_gather(query_row, "fsdp", axis=0, tiled=True)
    rows_local = w_key.shape[0]
    key_heads_local = w_key.reshape(rows_local, vit_heads, VHD)
    query_group = group_query.reshape(group_query.shape[0], vit_heads, VHD)
    key_part = jnp.einsum(
        "ihd,thd->thi", key_heads_local, query_group, preferred_element_type=jnp.float32
    )
    folded = lax.all_to_all(
        key_part.astype(jnp.bfloat16), "fsdp", split_axis=0, concat_axis=2, tiled=True
    ).astype(key_part.dtype)
    scores = jnp.einsum(
        "tpi,thi->thp", normed.astype(jnp.float32), folded, precision=lax.Precision.HIGHEST
    ) / math.sqrt(VHD)
    lifted = jnp.exp(scores)
    attn_probs = (lifted / jnp.sum(lifted, axis=-1, keepdims=True)).astype(jnp.bfloat16)
    mixed = jnp.einsum("thp,tpi->thi", attn_probs, normed, preferred_element_type=jnp.float32)
    spread_rows = lax.all_to_all(
        mixed.astype(jnp.bfloat16), "fsdp", split_axis=2, concat_axis=0, tiled=True
    ).astype(mixed.dtype)
    value_heads_local = w_value.reshape(rows_local, vit_heads, VHD).astype(jnp.float32)
    summed_heads = jnp.einsum(
        "thi,ihd->thd", spread_rows, value_heads_local, precision=lax.Precision.HIGHEST
    )
    pooled = lax.psum_scatter(
        summed_heads.reshape(tile_count * lax.axis_size("fsdp"), vit_width).astype(jnp.bfloat16),
        "fsdp",
        scatter_dimension=0,
        tiled=True,
    ).astype(jnp.float32)
    pooled = pooled.astype(jnp.bfloat16)
    class_input = tile_patches[:, 0, :].astype(jnp.float32)
    class_row = (
        class_input + jnp.dot(pooled, full_out, preferred_element_type=jnp.float32)
    ).astype(jnp.bfloat16)
    embeds = jnp.dot(class_row, full_proj, preferred_element_type=jnp.float32).astype(jnp.bfloat16)
    tile_slot = jnp.arange(tile_count, dtype=jnp.int32)
    present = (tile_slot < counts[0]).astype(jnp.int32)
    embeds = jnp.where(present[:, None] > 0, embeds, jnp.zeros_like(embeds))
    model_width = embeds.shape[1]
    rows_dev = tile_count * group_size
    total_tiles = rows_dev * seq_size
    segment = total_tiles // 4
    head_width = long_query.shape[1]
    heads_dev = head_width // (model_width // HEADS)
    leading_head = lax.axis_index("fsdp") * heads_dev
    targets = lax.axis_index("seq") * rows_dev + jnp.arange(rows_dev, dtype=jnp.int32)
    column_start = lax.axis_index("fsdp") * head_width
    all_embeds, all_order, all_present = (
        lax.all_gather(embeds, ("seq", "fsdp"), axis=0, tiled=True),
        lax.all_gather(seq_order, ("seq", "fsdp"), axis=0, tiled=True),
        lax.all_gather(present, ("seq", "fsdp"), axis=0, tiled=True),
    )
    picker = all_order[None, :] == targets[:, None]
    mine = jnp.dot(
        picker.astype(jnp.bfloat16), all_embeds, preferred_element_type=jnp.float32
    ).astype(jnp.bfloat16)
    mine_present = jnp.sum(jnp.where(picker, all_present[None, :], 0), axis=1).astype(jnp.int32)
    long_normed = layer_norm(mine, long_gain)
    query_rows = jnp.dot(long_normed, long_query, preferred_element_type=jnp.float32).astype(
        jnp.bfloat16
    )
    key_local = jnp.dot(long_normed, long_key, preferred_element_type=jnp.float32).astype(
        jnp.bfloat16
    )
    value_local = jnp.dot(long_normed, long_value, preferred_element_type=jnp.float32).astype(
        jnp.bfloat16
    )
    key_rows, value_rows, key_present = (
        lax.all_gather(key_local, "seq", axis=0, tiled=True),
        lax.all_gather(value_local, "seq", axis=0, tiled=True),
        lax.all_gather(mine_present, "seq", axis=0, tiled=True),
    )
    key_position_index = jnp.arange(total_tiles, dtype=jnp.int32)
    residual = lax.dynamic_slice_in_dim(mine, column_start, head_width, 1)
    attended = dilated_attention(
        query_rows,
        key_rows,
        value_rows,
        targets,
        key_position_index,
        key_present,
        leading_head,
        heads_dev,
        segment,
    )
    head_terms = jnp.dot(attended, long_out, preferred_element_type=jnp.float32)
    summed = lax.psum_scatter(
        head_terms.astype(jnp.bfloat16), "fsdp", scatter_dimension=1, tiled=True
    ).astype(jnp.float32)
    return (residual.astype(jnp.float32) + summed).astype(jnp.bfloat16)


def solution(mesh):
    return jax.shard_map(
        local,
        mesh=mesh,
        in_specs=(
            P(("group", "seq", "fsdp"), None, None),
            P(),
            P("fsdp", None),
            P("fsdp", None),
            P("fsdp", None),
            P("fsdp", None),
            P("fsdp", None),
            P(),
            P(None, "fsdp"),
            P(None, "fsdp"),
            P(None, "fsdp"),
            P("fsdp", None),
            P(("group", "seq", "fsdp")),
            P(("group", "seq", "fsdp")),
        ),
        out_specs=P(("group", "seq"), "fsdp"),
        check_vma=False,
    )
```

profile of v0, /device:TPU:0, one launch (start us, length us, event | category | flops | bytes accessed | tf_op | source)
XLA Modules:
  0.0 166.7 jit_solution(15862712524347487263)
XLA Ops:
  6.5 0.7 all-gather.6.cloned.1.call-update
  7.3 0.7 all-gather.10.cloned.1.call-update
  8.1 0.7 all-gather.8.cloned.1.call-update
  9.1 0.5 fusion.2
  10.3 0.5 fusion.4
  10.9 0.6 dynamic-slice
  12.3 2.1 %copy.37 = bf16[384,768]{0,1:T(8,128)(2,1)} copy(bf16[384,768]{1,0:T(8,128)(2,1)} %param.17) | data formatting | bytes 1179648 | tf_op args[3]
  14.4 0.6 dynamic-slice.2
  15.8 13.7 %all-reduce.4 = (s32[32]{0:T(128)S(1)}, s32[32]{0:T(128)S(1)}) all-reduce(s32[32]{0:T(128)S(1)} %dynamic-update-slice, s32[32]{0:T(128)S(1)} %fusion.55), channel_id=1, replica_groups=mesh['group'=2,'seq'=4,'fsdp'=4] {'seq','fsdp'}, use_global_device_ids=true, to_apply=%add | all-reduce | flops 64 | bytes 512
  30.0 6.2 %all-reduce.2 = s32[32]{0:T(128)S(1)} all-reduce(s32[32]{0:T(128)S(1)} %dynamic-update-slice.2), channel_id=1, replica_groups=mesh['group'=2,'seq'=4,'fsdp'=4] {'seq'}, use_global_device_ids=true, to_apply=%add.2 | all-reduce | flops 32 | bytes 256
  36.5 2.1 %fusion.17 = bf16[1,2,768]{2,1,0:T(2,128)(2,1)S(1)} fusion(bf16[1536,768]{1,0:T(8,128)(2,1)} %all-gather.6.cloned.1.call-done, bf16[2,1,1536]{2,1,0:T(2,128)(2,1)S(1)} %slice.8), kind=kOutput, calls=%fused_computation.32 | convolution fusion | flops 4720128 | bytes 2368512 | tf_op jit(solution)/shard_map/dot_general | solution.py:103
  38.6 5.2 %all-gather = bf16[4,2,768]{2,1,0:T(2,128)(2,1)S(1)} all-gather(bf16[1,2,768]{2,1,0:T(2,128)(2,1)S(1)} %fusion.17), channel_id=1, replica_groups=mesh['group'=2,'seq'=4,'fsdp'=4] {'fsdp'}, dimensions={0}, use_global_device_ids=true | all-gather | bytes 15360 | tf_op jit(solution)/shard_map/all_gather | solution.py:106
  44.1 0.7 copy.39
  44.7 3.3 %all-to-all-start = ((bf16[8,12,384]{2,1,0:T(8,128)(2,1)}), bf16[8,12,384]{2,1,0:T(8,128)(2,1)S(1)}, u32[]{:S(2)}, u32[]{:S(2)}) async-start(bf16[8,12,384]{2,1,0:T(8,128)(2,1)} %copy.39), calls=%async_computation | async-start | bytes 196608 | tf_op jit(solution)/shard_map/all_to_all | solution.py:113
  48.1 5.5 %all-to-all-done = bf16[8,12,384]{2,1,0:T(8,128)(2,1)S(1)} async-done(((bf16[8,12,384]{2,1,0:T(8,128)(2,1)}), bf16[8,12,384]{2,1,0:T(8,128)(2,1)S(1)}, u32[]{:S(2)}, u32[]{:S(2)}) %all-to-all-start) | async-done | bytes 73760 | tf_op jit(solution)/shard_map/all_to_all | solution.py:113
  54.7 0.6 copy.42
  55.3 2.1 %reshape.362 = bf16[4,2,4608]{2,1,0:T(2,128)(2,1)} reshape(bf16[1536,2,12]{2,1,0:T(2,128)(2,1)S(1)} %bitcast.61) | data formatting | bytes 147456
  57.4 3.3 %all-to-all-start.1 = ((bf16[4,2,4608]{2,1,0:T(2,128)(2,1)}), bf16[4,2,4608]{2,1,0:T(2,128)(2,1)S(1)}, u32[]{:S(2)}, u32[]{:S(2)}) async-start(bf16[4,2,4608]{2,1,0:T(2,128)(2,1)} %reshape.362), calls=%async_computation.1 | async-start | bytes 147456 | tf_op jit(solution)/shard_map/all_to_all | solution.py:122
  61.1 0.6 dynamic-slice.3
  62.4 2.5 %all-to-all-done.1 = bf16[4,2,4608]{2,1,0:T(2,128)(2,1)S(1)} async-done(((bf16[4,2,4608]{2,1,0:T(2,128)(2,1)}), bf16[4,2,4608]{2,1,0:T(2,128)(2,1)S(1)}, u32[]{:S(2)}, u32[]{:S(2)}) %all-to-all-start.1) | async-done | bytes 73760 | tf_op jit(solution)/shard_map/all_to_all | solution.py:122
  64.8 1.8 %reshape.363 = bf16[1536,2,12]{2,1,0:T(2,128)(2,1)S(1)} reshape(bf16[4,2,4608]{2,1,0:T(2,128)(2,1)S(1)} %all-to-all-done.1) | data formatting | bytes 147456
  66.7 0.6 copy.52
  67.8 10.6 %all-reduce.3 = bf16[8,768]{1,0:T(8,128)(2,1)S(1)} all-reduce(bf16[8,768]{1,0:T(8,128)(2,1)S(1)} %convert_element_type.110), channel_id=2, replica_groups=mesh['group'=2,'seq'=4,'fsdp'=4] {'fsdp'}, use_global_device_ids=true, to_apply=%region_3.0.clone | all-reduce | flops 6144 | bytes 24576
  78.5 9.8 %all-gather.8.cloned.1.call-done = bf16[768,1536]{1,0:T(8,128)(2,1)} async-done(((bf16[192,1536]{1,0:T(8,128)(2,1)}), bf16[768,1536]{1,0:T(8,128)(2,1)}) %all-gather.8.cloned.1.call-update) | async-done | bytes 2359312 | tf_op jit(solution)/shard_map/all_gather | solution.py:100
  88.3 3.2 %fusion.16 = bf16[1,2,768]{2,1,0:T(2,128)(2,1)S(1)} fusion(bf16[1536,768]{1,0:T(8,128)(2,1)} %all-gather.10.cloned.1.call-done, bf16[768,1536]{1,0:T(8,128)(2,1)} %all-gather.8.cloned.1.call-done, f32[2,1,1536]{2,1,0:T(1,128)S(1)} %slice_convert_fusion, pred[2]{0:T(512)(128)(4,1)S(1)} %fusion.56, bf16[8,768]{1,0:T(8,128)(2,1)S(1)} %all-reduce.3, ...), kind=kOutput, calls=%fused_computation.31 | convolution fusion | flops 9446400 | bytes 4737540 | tf_op jit(solution)/shard_map/dot_general | solution.py:140
  91.5 20.5 %all-gather.1 = bf16[16,2,768]{2,1,0:T(2,128)(2,1)S(1)} all-gather(bf16[1,2,768]{2,1,0:T(2,128)(2,1)S(1)} %fusion.16), channel_id=1, replica_groups=mesh['group'=2,'seq'=4,'fsdp'=4] {'seq','fsdp'}, dimensions={0}, use_global_device_ids=true | all-gather | bytes 52224 | tf_op jit(solution)/shard_map/all_gather | solution.py:154
  113.1 13.2 %all_gather.39 = bf16[32,192]{1,0:T(8,128)(2,1)S(1)} all-gather(bf16[8,192]{1,0:T(8,128)(2,1)S(1)} %convolution_convert_fusion.5), channel_id=1, replica_groups=mesh['group'=2,'seq'=4,'fsdp'=4] {'seq'}, dimensions={0}, use_global_device_ids=true | all-gather | bytes 15360 | tf_op jit(solution)/shard_map/all_gather | solution.py:174
  126.6 13.2 %all_gather.36 = bf16[32,192]{1,0:T(8,128)(2,1)S(1)} all-gather(bf16[8,192]{1,0:T(8,128)(2,1)S(1)} %convolution_convert_fusion.7), channel_id=1, replica_groups=mesh['group'=2,'seq'=4,'fsdp'=4] {'seq'}, dimensions={0}, use_global_device_ids=true | all-gather | bytes 15360 | tf_op jit(solution)/shard_map/all_gather | solution.py:175
  140.7 0.8 copy.53
  141.5 17.1 %reduce-scatter.4.cloned.1.call-done = bf16[192,8]{1,0:T(8,128)(2,1)} async-done(((bf16[768,8]{1,0:T(8,128)(2,1)}), bf16[192,8]{1,0:T(8,128)(2,1)}) %reduce-scatter.4.cloned.1.call-update) | async-done | bytes 3088
  158.6 0.8 copy.54
  159.5 0.7 add_convert_fusion
  (86 shorter events, 5.7 us)
Async XLA Ops:
  6.5 134.0 %copy-start = (bf16[192,768]{1,0:T(8,128)(2,1)S(1)}, bf16[192,768]{1,0:T(8,128)(2,1)}, u32[]{:S(2)}) copy-start(bf16[192,768]{1,0:T(8,128)(2,1)} %param.25) | copy-start | bytes 884740
  6.5 2.2 %copy-start.1 = (bf16[2,256,1536]{2,1,0:T(8,128)(2,1)S(1)}, bf16[2,256,1536]{2,1,0:T(8,128)(2,1)}, u32[]{:S(2)}) copy-start(bf16[2,256,1536]{2,1,0:T(8,128)(2,1)} %param.14) | copy-start | bytes 4718596
  6.5 3.8 %copy-start.4 = (f32[1536]{0:T(1024)S(1)}, f32[1536]{0:T(1024)}, u32[]{:S(2)}) copy-start(f32[1536]{0:T(1024)} %param.15) | copy-start | bytes 18436
  6.5 29.9 %all-gather.6.cloned.1.call-start = ((), (), s32[]{:S(2)}) async-start(), calls=%async_computation.3 | async-start | bytes 2949120 | tf_op jit(solution)/shard_map/all_gather | solution.py:99
  7.3 71.2 %all-gather.10.cloned.1.call-start = ((), (), s32[]{:S(2)}) async-start(), calls=%async_computation.5 | async-start | bytes 2949120 | tf_op jit(solution)/shard_map/all_gather | solution.py:101
  8.0 80.3 %all-gather.8.cloned.1.call-start = ((), (), s32[]{:S(2)}) async-start(), calls=%async_computation.4 | async-start | bytes 2949120 | tf_op jit(solution)/shard_map/all_gather | solution.py:100
  9.1 1.8 %copy-start.12 = (u32[32]{0:T(128)S(1)}, u32[32]{0:T(128)}, u32[]{:S(2)}) copy-start(u32[32]{0:T(128)} %constant.98) | copy-start | bytes 388
  9.6 4.8 %copy-start.11 = (u32[32]{0:T(128)S(1)}, u32[32]{0:T(128)}, u32[]{:S(2)}) copy-start(u32[32]{0:T(128)} %constant.108) | copy-start | bytes 388
  9.6 5.4 %copy-start.9 = (s32[2]{0:T(128)S(1)}, s32[2]{0:T(128)}, u32[]{:S(2)}) copy-start(s32[2]{0:T(128)} %param.26) | copy-start | bytes 28
  36.4 7.4 %copy-start.2 = (bf16[384,768]{0,1:T(8,128)(2,1)S(1)}, bf16[384,768]{0,1:T(8,128)(2,1)}, u32[]{:S(2)}) copy-start(bf16[384,768]{0,1:T(8,128)(2,1)} %copy.37) | copy-start | bytes 1769476
  44.7 8.9 %all-to-all-start = ((bf16[8,12,384]{2,1,0:T(8,128)(2,1)}), bf16[8,12,384]{2,1,0:T(8,128)(2,1)S(1)}, u32[]{:S(2)}, u32[]{:S(2)}) async-start(bf16[8,12,384]{2,1,0:T(8,128)(2,1)} %copy.39), calls=%async_computation | async-start | bytes 196608 | tf_op jit(solution)/shard_map/all_to_all | solution.py:113
  53.7 7.1 %copy-start.3 = (bf16[384,768]{1,0:T(8,128)(2,1)S(1)}, bf16[384,768]{1,0:T(8,128)(2,1)}, u32[]{:S(2)}) copy-start(bf16[384,768]{1,0:T(8,128)(2,1)} %param.18) | copy-start | bytes 1769476
  54.3 6.8 %copy-start.10 = (u32[32]{0:T(128)S(1)}, u32[32]{0:T(128)}, u32[]{:S(2)}) copy-start(u32[32]{0:T(128)} %constant.116) | copy-start | bytes 388
  57.4 7.4 %all-to-all-start.1 = ((bf16[4,2,4608]{2,1,0:T(2,128)(2,1)}), bf16[4,2,4608]{2,1,0:T(2,128)(2,1)S(1)}, u32[]{:S(2)}, u32[]{:S(2)}) async-start(bf16[4,2,4608]{2,1,0:T(2,128)(2,1)} %reshape.362), calls=%async_computation.1 | async-start | bytes 147456 | tf_op jit(solution)/shard_map/all_to_all | solution.py:122
  60.7 97.9 %reduce-scatter.4.cloned.1.call-start = ((), (), s32[]{:S(2)}) async-start(), calls=%async_computation.6 | async-start | bytes 245760
  78.4 34.2 %copy-start.5 = (bf16[768,192]{0,1:T(8,128)(2,1)S(1)}, bf16[768,192]{0,1:T(8,128)(2,1)}, u32[]{:S(2)}) copy-start(bf16[768,192]{0,1:T(8,128)(2,1)} %param.22) | copy-start | bytes 884740
  78.4 34.2 %copy-start.8 = (f32[768]{0:T(1024)S(1)}, f32[768]{0:T(1024)}, u32[]{:S(2)}) copy-start(f32[768]{0:T(1024)} %param.21) | copy-start | bytes 9220
  78.4 34.4 %copy-start.6 = (bf16[768,192]{0,1:T(8,128)(2,1)S(1)}, bf16[768,192]{0,1:T(8,128)(2,1)}, u32[]{:S(2)}) copy-start(bf16[768,192]{0,1:T(8,128)(2,1)} %param.23) | copy-start | bytes 884740
  78.5 47.9 %copy-start.7 = (bf16[768,192]{0,1:T(8,128)(2,1)S(1)}, bf16[768,192]{0,1:T(8,128)(2,1)}, u32[]{:S(2)}) copy-start(bf16[768,192]{0,1:T(8,128)(2,1)} %param.24) | copy-start | bytes 884740
Sparse Core Ops, SparseCore 0:
  8.9 26.8 all-gather.5
  37.3 25.1 all-gather.9
  64.1 24.1 all-gather.7
  141.6 16.9 reduce-scatter.3
where the time goes:
time: 167 us
  blocking collectives  82.6 us (49%)
  waiting for transfers between devices  37.1 us (22%)
  between operations  16.1 us (10%)
  local copies, waits for them, and re-layouts  13 us (8%)
  matrix products  8.25 us (5%)
  starting transfers between devices  6.71 us (4%)
  other arithmetic  2.85 us (2%)
    unnamed x3, blocking collectives  30.5 us
    all_gather x1, blocking collectives, local(): lax.all_gather(embeds, ('seq', 'fsdp'), axis=0, tiled=True)  20.5 us
    unnamed x5, waiting for transfers between devices  19.2 us
    all_gather x1, blocking collectives, local(): lax.all_gather(key_local, 'seq', axis=0, tiled=True)  13.2 us
    all_gather x1, blocking collectives, local(): lax.all_gather(value_local, 'seq', axis=0, tiled=True)  13.2 us
    unnamed x41, local copies, waits for them, and re-layouts  10.4 us
    all_gather x1, waiting for transfers between devices, local(): lax.all_gather(w_out, 'fsdp', axis=0, tiled=True)  9.84 us
    all_to_all x1, waiting for transfers between devices, local(): lax.all_to_all(key_part.astype(jnp.bfloat16), 'fsdp', split_axis=0, conca...  5.54 us
  transfers between devices with their start and end apart: 6, of which 4 were waited for; matrix products, arithmetic and copies ran while one was open for 10% of the time, Pallas kernels for 0%

commit v1 on v0

v1 whole, which is shorter than its diff:
```python
import functools
import math

import jax
import jax.numpy as jnp
from jax import lax
from jax.experimental import pallas as pl
from jax.experimental.pallas import tpu as pltpu
from jax.sharding import PartitionSpec as P

VHD = 64
HEADS = 16
DILATION_STEP = 4
EPSILON = 1e-06
LN_ROWS = 32

F32 = jnp.float32
BF16 = jnp.bfloat16


def up(n, m):
    return (n + m - 1) // m * m


def norm_rows(x, gain):
    mean = jnp.mean(x, axis=-1, keepdims=True)
    centred = x - mean
    variance = jnp.mean(centred * centred, axis=-1, keepdims=True)
    return centred * lax.rsqrt(variance + EPSILON) * gain


def dot(a, b):
    return jnp.dot(a, b, preferred_element_type=F32)


def dot_t(a, b):
    return lax.dot_general(a, b, (((1,), (1,)), ((), ())), preferred_element_type=F32)


def kernel(
    F, S,
    patches, vit_gain, w_query, w_key, w_value, w_out, w_proj,
    long_gain, long_query, long_key, long_value, long_out, order, counts,
    out,
    cls, xbuf, normed, wq, wk, wv, wo, wp, lq, lk, lv, lo,
    s1, r1, sm, rm, sm2, rm2, s2, r2, s3, r3, s4, r4, s5, r5, s6, r6, s7, r7,
    s8, r8, s9, r9, qbuf, seqc,
    lsem, fsend, frecv, zsend, zrecv,
):
    T, PATCH, DV = patches.shape
    VW = w_key.shape[1]
    D = w_proj.shape[1]
    R = T * F
    N = R * S
    C = DV // F
    HC = long_query.shape[1]
    OC = D // F
    PC = VW // F
    HP = up(VW // VHD, 16)
    f = lax.axis_index("fsdp")
    z = lax.axis_index("seq")

    loads = []

    def load(src, dst):
        c = pltpu.make_async_copy(src, dst, lsem.at[len(loads)])
        c.start()
        loads.append(c)
        return c

    ld_cls = load(patches.at[:, pl.ds(0, 16), :], cls)
    barrier = pltpu.get_barrier_semaphore()
    for k in range(1, F):
        pl.semaphore_signal(
            barrier, inc=1, device_id={"fsdp": lax.rem(f + k, F)},
            device_id_type=pl.DeviceIdType.MESH)
    for k in range(1, S):
        pl.semaphore_signal(
            barrier, inc=1, device_id={"seq": lax.rem(z + k, S)},
            device_id_type=pl.DeviceIdType.MESH)
    ld_wq = load(w_query, wq)
    ld_x = [load(patches.at[t], xbuf.at[t]) for t in range(T)]
    ld_wk = load(w_key, wk)
    ld_wv = load(w_value, wv)
    ld_wo = load(w_out, wo)
    ld_wp = load(w_proj, wp)
    ld_lq = load(long_query, lq)
    ld_lk = load(long_key, lk)
    ld_lv = load(long_value, lv)
    ld_lo = load(long_out, lo)

    sends = []

    def push(hop, axis, me, n, src, dst, send_sems, recv_sems):
        for k in sorted(range(1, n), key=lambda k: abs(2 * k - n)):
            peer = lax.rem(me + k, n)
            c = pltpu.make_async_remote_copy(
                src_ref=src(peer), dst_ref=dst.at[me],
                send_sem=send_sems.at[hop, k], recv_sem=recv_sems.at[hop, me],
                device_id={axis: peer}, device_id_type=pl.DeviceIdType.MESH)
            c.start()
            sends.append(c)

    def collect(hop, axis, me, n, dst, send_sems, recv_sems):
        for k in range(1, n):
            peer = lax.rem(me + k, n)
            pltpu.make_async_remote_copy(
                src_ref=dst.at[me], dst_ref=dst.at[peer],
                send_sem=send_sems.at[hop, k], recv_sem=recv_sems.at[hop, peer],
                device_id={axis: peer}, device_id_type=pl.DeviceIdType.MESH,
            ).wait_recv()

    def scatter(hop, src, dst):
        push(hop, "fsdp", f, F, lambda peer: src.at[peer], dst, fsend, frecv)
        dst[f] = src[f]

    def spread(hop, src, dst):
        push(hop, "fsdp", f, F, lambda peer: src, dst, fsend, frecv)
        dst[f] = src[...]

    def spread_z(hop, src, dst):
        push(hop, "seq", z, S, lambda peer: src, dst, zsend, zrecv)
        dst[z] = src[...]

    def arrive(hop, dst):
        collect(hop, "fsdp", f, F, dst, fsend, frecv)

    def arrive_z(hop, dst):
        collect(hop, "seq", z, S, dst, zsend, zrecv)

    def total(ref, n):
        acc = ref[0]
        for j in range(1, n):
            acc = acc + ref[j]
        return acc

    L = sm.shape[1]
    lane = lax.broadcasted_iota(jnp.int32, sm.shape, 1)
    row = lax.broadcasted_iota(jnp.int32, sm.shape, 0)
    meta = jnp.zeros(sm.shape, jnp.int32)
    first = z * R + f * T
    for t in range(T):
        here = jnp.where(t < counts[0], 1, 0)
        value = jnp.where(row == 0, order[t] + 1, jnp.where(row == 1, here, 0))
        meta = jnp.where(lane == first + t, value, meta)
    sm[...] = meta

    ld_cls.wait()
    raw = jnp.concatenate([cls[t, 0:8, :].astype(F32)[0:1] for t in range(T)], axis=0)
    class_normed = norm_rows(raw, vit_gain[...]).astype(BF16).astype(F32)
    filler = s1.shape[1] - 2 * T
    packed = jnp.concatenate(
        [class_normed, raw, jnp.zeros((filler, DV), F32)], axis=0)
    for j in range(F):
        s1[j] = packed[:, j * C:(j + 1) * C]
    pl.semaphore_wait(barrier, F - 1 + S - 1)
    scatter(0, s1, r1)
    spread(1, sm, rm)

    blocks = PATCH // LN_ROWS

    def norm_blocks(lo_block, hi_block):
        def body(i, carry):
            t = i // blocks
            start = pl.multiple_of((i % blocks) * LN_ROWS, LN_ROWS)
            x = xbuf[t, pl.ds(start, LN_ROWS), :].astype(F32)
            y = norm_rows(x, vit_gain[...])
            for j in range(F):
                normed[t, j, pl.ds(start, LN_ROWS), :] = y[:, j * C:(j + 1) * C].astype(BF16)
            return carry
        lax.fori_loop(lo_block, hi_block, body, 0)

    third = T * blocks // 3
    for c in ld_x:
        c.wait()
    norm_blocks(0, third)

    ld_wq.wait()
    arrive(0, r1)
    xq = jnp.concatenate([r1[j][0:T] for j in range(F)], axis=0)
    s2[...] = dot(xq.astype(BF16), wq[...])
    spread(2, s2, r2)
    arrive(1, rm)
    sm2[...] = total(rm, F)
    spread_z(0, sm2, rm2)
    norm_blocks(third, 2 * third)
    ld_wk.wait()
    arrive(2, r2)
    query = total(r2, F).astype(BF16).astype(F32)

    head = lax.broadcasted_iota(jnp.int32, (R, HP, VW), 1)
    column = lax.broadcasted_iota(jnp.int32, (R, HP, VW), 2)
    own_head = (column >= head * VHD) & (column < (head + 1) * VHD)
    spread_query = jnp.where(own_head, query[:, None, :], 0.0).reshape(R * HP, VW)
    folded = dot_t(spread_query.astype(BF16), wk[...]).astype(BF16)
    s3[...] = folded.reshape(F, T * HP, C)
    scatter(3, s3, r3)
    norm_blocks(2 * third, T * blocks)
    arrive(3, r3)

    for t in range(T):
        scores = dot_t(r3[0, pl.ds(t * HP, HP), :], normed[t, 0])
        for j in range(1, F):
            scores = scores + dot_t(r3[j, pl.ds(t * HP, HP), :], normed[t, j])
        lifted = jnp.exp(scores / math.sqrt(VHD))
        probs = (lifted / jnp.sum(lifted, axis=-1, keepdims=True)).astype(BF16)
        for j in range(F):
            s4[j, pl.ds(t * HP, HP), :] = dot(probs, normed[t, j]).astype(BF16)
    scatter(4, s4, r4)
    ld_wv.wait()
    ld_wo.wait()
    arrive(4, r4)

    summed = dot(r4[...].reshape(R * HP, C), wv[...]).reshape(R, HP, VW)
    pooled_part = jnp.sum(jnp.where(own_head, summed, 0.0), axis=1)
    for j in range(F):
        s5[j] = pooled_part[:, j * PC:(j + 1) * PC]
    scatter(5, s5, r5)
    arrive(5, r5)
    pooled = total(r5, F).astype(BF16)
    row_part = dot(pooled, wo[...])
    for j in range(F):
        s6[j] = row_part[:, j * C:(j + 1) * C]
    scatter(6, s6, r6)
    class_raw = jnp.concatenate([r1[j][T:2 * T] for j in range(F)], axis=0)
    ld_wp.wait()
    arrive(6, r6)
    class_row = (class_raw + total(r6, F)).astype(BF16)
    s7[...] = dot(class_row, wp[...])
    spread(7, s7, r7)

    arrive_z(0, rm2)
    all_meta = total(rm2, S)
    all_order = all_meta[0:1, 0:N]
    all_present = all_meta[1:2, 0:N].astype(F32)
    position = lax.broadcasted_iota(jnp.int32, (N, N), 0) + 1
    picker = jnp.where(position == all_order, 1.0, 0.0)
    picker_tissue = (picker * all_present).astype(BF16)
    key_present = dot_t(jnp.broadcast_to(all_present, (8, N)).astype(BF16), picker.astype(BF16))[0:1]

    arrive(7, r7)
    embeds = total(r7, F).astype(BF16).astype(F32)
    half = D // 2
    s8[...] = jnp.concatenate([embeds[:, :half], embeds[:, half:]], axis=0).astype(BF16)
    spread_z(1, s8, r8)
    heads_dev = HC // (D // HEADS)
    hw = D // HEADS
    hr = (heads_dev, R, N)
    m_head = lax.broadcasted_iota(jnp.int32, hr, 0) + f * heads_dev
    m_row = lax.broadcasted_iota(jnp.int32, hr, 1) + z * R
    m_key = lax.broadcasted_iota(jnp.int32, hr, 2)
    segment = N // 4
    allowed = (key_present.reshape(1, 1, N) > 0.5) | (m_row == m_key)
    in_local = m_row // segment == m_key // segment
    in_dilated = (m_row % DILATION_STEP == m_head % DILATION_STEP) & (
        m_key % DILATION_STEP == m_head % DILATION_STEP)
    times = jnp.where(
        allowed, jnp.where(in_local, 1.0, 0.0) + jnp.where(in_dilated, 1.0, 0.0), 0.0
    ).reshape(heads_dev * R, N)
    a_head = lax.broadcasted_iota(jnp.int32, (heads_dev, R, HC), 0)
    a_col = lax.broadcasted_iota(jnp.int32, (heads_dev, R, HC), 2)
    mine = (a_col >= a_head * hw) & (a_col < (a_head + 1) * hw)
    ld_lq.wait()
    ld_lk.wait()
    ld_lv.wait()
    ld_lo.wait()
    arrive_z(1, r8)

    left = jnp.concatenate([r8[j].astype(F32)[:R] for j in range(S)], axis=0)
    right = jnp.concatenate([r8[j].astype(F32)[R:] for j in range(S)], axis=0)
    every = jnp.concatenate([left, right], axis=1).astype(BF16)
    sequence = dot(picker_tissue, every)
    lnormed = norm_rows(sequence, long_gain[...]).astype(BF16)
    qbuf[...] = dot(lnormed, lq[...])
    keys = dot(lnormed, lk[...]).astype(BF16)
    values = dot(lnormed, lv[...]).astype(BF16)
    queries = qbuf[pl.ds(pl.multiple_of(z * R, R), R), :].astype(BF16).astype(F32)
    per_head = jnp.where(mine, queries[None], 0.0).reshape(heads_dev * R, HC).astype(BF16)
    lifted = jnp.exp(dot_t(per_head, keys) / math.sqrt(hw))
    weights = lifted.astype(BF16).astype(F32) * times
    denominator = jnp.sum(lifted * times, axis=-1, keepdims=True)
    mixed = dot(weights.astype(BF16), values) / denominator
    attended = jnp.sum(
        jnp.where(mine, mixed.reshape(heads_dev, R, HC), 0.0), axis=0).astype(BF16)
    terms = dot(attended, lo[...])
    for j in range(F):
        s9[j] = terms[:, j * OC:(j + 1) * OC]
    scatter(8, s9, r9)
    for j in range(F):
        seqc[j] = sequence[:, j * OC:(j + 1) * OC]
    residual = seqc[f, pl.ds(pl.multiple_of(z * R, R), R), :]
    arrive(8, r9)
    out[...] = (residual + total(r9, F)).astype(BF16)
    for c in sends:
        c.wait_send()


def local(
    tile_patches, vit_gain, w_query, w_key, w_value, w_out, w_proj,
    long_gain, long_query, long_key, long_value, long_out, seq_order, counts,
):
    S = lax.axis_size("seq")
    F = lax.axis_size("fsdp")
    T, PATCH, DV = tile_patches.shape
    VW = w_key.shape[1]
    D = w_proj.shape[1]
    R, C, HC, OC, PC = T * F, DV // F, long_query.shape[1], D // F, VW // F
    HP = up(VW // VHD, 16)
    N = R * S
    L = up(N, 128)
    V = pltpu.VMEM
    any_, vmem, smem = (
        pl.BlockSpec(memory_space=m) for m in (pl.ANY, pltpu.VMEM, pltpu.SMEM))
    like = lambda a: V(a.shape, a.dtype)
    pair = lambda shape, dtype: [V((F,) + shape, dtype), V((F,) + shape, dtype)]
    fan = lambda n, shape, dtype: [V(shape, dtype), V((n,) + shape, dtype)]
    flops = 2 * (3 * R * HP * C * VW + 2 * T * HP * PATCH * DV + 3 * N * D * HC)
    return pl.pallas_call(
        functools.partial(kernel, F, S),
        out_shape=jax.ShapeDtypeStruct((R, OC), BF16),
        in_specs=[any_, vmem, any_, any_, any_, any_, any_, vmem,
                  any_, any_, any_, any_, smem, smem],
        out_specs=vmem,
        scratch_shapes=[
            V((T, 16, DV), BF16), like(tile_patches), V((T, F, PATCH, C), BF16),
            like(w_query), like(w_key), like(w_value), like(w_out), like(w_proj),
            like(long_query), like(long_key), like(long_value), like(long_out),
            *pair((up(2 * T, 8), C), F32),
            *fan(F, (8, L), jnp.int32),
            *fan(S, (8, L), jnp.int32),
            *fan(F, (R, VW), F32),
            *pair((T * HP, C), BF16),
            *pair((T * HP, C), BF16),
            *pair((R, PC), F32),
            *pair((R, C), F32),
            *fan(F, (R, D), F32),
            *fan(S, (2 * R, D // 2), BF16),
            *pair((R, OC), F32),
            V((N, HC), F32), V((F, N, OC), F32),
            pltpu.SemaphoreType.DMA((10 + T,)),
            pltpu.SemaphoreType.DMA((9, F)), pltpu.SemaphoreType.DMA((9, F)),
            pltpu.SemaphoreType.DMA((2, S)), pltpu.SemaphoreType.DMA((2, S)),
        ],
        compiler_params=pltpu.CompilerParams(
            collective_id=0, has_side_effects=True, vmem_limit_bytes=48 * 2**20),
        cost_estimate=pl.CostEstimate(
            flops=flops, bytes_accessed=8 * 2**20, transcendentals=T * HP * PATCH),
    )(
        tile_patches, vit_gain.reshape(1, DV), w_query, w_key, w_value, w_out, w_proj,
        long_gain.reshape(1, D), long_query, long_key, long_value, long_out,
        seq_order, counts,
    )


def solution(mesh):
    return jax.shard_map(
        local,
        mesh=mesh,
        in_specs=(
            P(("group", "seq", "fsdp"), None, None),
            P(),
            P("fsdp", None),
            P("fsdp", None),
            P("fsdp", None),
            P("fsdp", None),
            P("fsdp", None),
            P(),
            P(None, "fsdp"),
            P(None, "fsdp"),
            P(None, "fsdp"),
            P("fsdp", None),
            P(("group", "seq", "fsdp")),
            P(("group", "seq", "fsdp")),
        ),
        out_specs=P(("group", "seq"), "fsdp"),
        check_vma=False,
    )
```

time: 167 us -> 48.3 us (0.29)
  blocking collectives: 82.6 us -> 0 us
  waiting for transfers between devices: 37.1 us -> 0 us
  Pallas kernels: 0 us -> 36.2 us
  between operations: 16.1 us -> 0.85 us
  matrix products: 8.25 us -> 0 us
  starting transfers between devices: 6.71 us -> 0 us
  other arithmetic: 2.85 us -> 0 us
  local copies, waits for them, and re-layouts: 13 us -> 10.7 us
    all_gather x4 -> x0, blocking collectives: 52.1 us -> none  [the longest x1 20.5 us: local(): lax.all_gather(embeds, ('seq', 'fsdp'), axis=0, tiled=True)]
    pallas_call x0 -> x1, Pallas kernels: none -> 36.2 us  [local(): pl.pallas_call(functools.partial(kernel, F, S), out_shape=jax.ShapeDtypeS...]
    unnamed x3 -> x0, blocking collectives: 30.5 us -> none
    unnamed x5 -> x0, waiting for transfers between devices: 19.2 us -> none
    all_gather x3 -> x0, waiting for transfers between devices: 9.88 us -> none  [the longest x1 9.84 us: local(): lax.all_gather(w_out, 'fsdp', axis=0, tiled=True)]
    dot_general x14 -> x0, matrix products: 8.25 us -> none  [the longest x1 3.2 us: local(): jnp.dot(class_row, full_proj, preferred_element_type=jnp.float32)]
    all_to_all x2 -> x0, waiting for transfers between devices: 8.03 us -> none  [the longest x1 5.54 us: local(): lax.all_to_all(key_part.astype(jnp.bfloat16), 'fsdp', split_axis=0, conca...]
    all_to_all x2 -> x0, starting transfers between devices: 6.59 us -> none  [the longest x1 3.3 us: local(): lax.all_to_all(key_part.astype(jnp.bfloat16), 'fsdp', split_axis=0, conca...]
  transfers between devices with their start and end apart: 6 -> 0, of which waited for: 4 -> 0; matrix products, arithmetic and copies ran while one was open for 10% -> 0% of each run, Pallas kernels for 0% -> 0%
where the time goes in v1:
time: 48.3 us; the launch traced here: 47.8 us
  Pallas kernels  36.2 us (75%)
  local copies, waits for them, and re-layouts  10.7 us (22%)
  between operations  0.85 us (2%)
    pallas_call x1, Pallas kernels, local(): pl.pallas_call(functools.partial(kernel, F, S), out_shape=jax.ShapeDtypeS...  36.2 us
    unnamed x20, local copies, waits for them, and re-layouts  9.31 us

profile of v1, /device:TPU:0, one launch (start us, length us, event | category | flops | bytes accessed | tf_op | source)
XLA Modules:
  0.0 47.8 jit_solution(15125702973614123070)
XLA Ops:
  0.0 0.0 copy-start.7
  0.0 0.0 copy-start.6
  0.0 0.0 copy-start
  0.8 0.7 %reshape.7.long_gain = f32[1,768]{1,0:T(1,128)S(1)} reshape(f32[768]{0:T(1024)} %param.21) | data formatting | bytes 6144 | tf_op jit(solution)/shard_map/reshape | solution.py:350
  1.5 0.7 %reshape.6.vit_gain = f32[1,1536]{1,0:T(1,128)S(1)} reshape(f32[1536]{0:T(1024)} %param.15) | data formatting | bytes 12288 | tf_op jit(solution)/shard_map/reshape | solution.py:349
  2.2 1.1 %copy.15.long_query = bf16[768,192]{1,0:T(8,128)(2,1)S(1)} copy(bf16[768,192]{0,1:T(8,128)(2,1)} %param.22) | data formatting | bytes 589824 | tf_op args[8]
  3.3 1.1 %copy.16.long_key = bf16[768,192]{1,0:T(8,128)(2,1)S(1)} copy(bf16[768,192]{0,1:T(8,128)(2,1)} %param.23) | data formatting | bytes 589824 | tf_op args[9]
  4.5 1.1 %copy.17.long_value = bf16[768,192]{1,0:T(8,128)(2,1)S(1)} copy(bf16[768,192]{0,1:T(8,128)(2,1)} %param.24) | data formatting | bytes 589824 | tf_op args[10]
  5.6 0.0 copy-done.7
  5.6 0.0 copy-done.6
  5.6 0.0 copy-done
  5.6 0.0 copy-start.1
  5.6 1.1 %copy-done.1 = bf16[384,768]{1,0:T(8,128)(2,1)S(1)} copy-done((bf16[384,768]{1,0:T(8,128)(2,1)S(1)}, bf16[384,768]{1,0:T(8,128)(2,1)}, u32[]{:S(2)}) %copy-start.1) | copy-done | bytes 589848
  6.7 0.0 copy-start.2
  6.7 1.1 %copy-done.2 = bf16[384,768]{1,0:T(8,128)(2,1)S(1)} copy-done((bf16[384,768]{1,0:T(8,128)(2,1)S(1)}, bf16[384,768]{1,0:T(8,128)(2,1)}, u32[]{:S(2)}) %copy-start.2) | copy-done | bytes 589848
  7.8 0.0 copy-start.3
  7.8 1.1 %copy-done.3 = bf16[384,768]{1,0:T(8,128)(2,1)S(1)} copy-done((bf16[384,768]{1,0:T(8,128)(2,1)S(1)}, bf16[384,768]{1,0:T(8,128)(2,1)}, u32[]{:S(2)}) %copy-start.3) | copy-done | bytes 589848
  8.8 0.0 copy-start.4
  8.8 1.1 %copy-done.4 = bf16[192,1536]{1,0:T(8,128)(2,1)S(1)} copy-done((bf16[192,1536]{1,0:T(8,128)(2,1)S(1)}, bf16[192,1536]{1,0:T(8,128)(2,1)}, u32[]{:S(2)}) %copy-start.4) | copy-done | bytes 589848
  9.9 0.0 copy-start.5
  9.9 1.1 %copy-done.5 = bf16[384,768]{1,0:T(8,128)(2,1)S(1)} copy-done((bf16[384,768]{1,0:T(8,128)(2,1)S(1)}, bf16[384,768]{1,0:T(8,128)(2,1)}, u32[]{:S(2)}) %copy-start.5) | copy-done | bytes 589848
  11.0 36.2 %shard_map.136 = bf16[8,192]{1,0:T(8,128)(2,1)S(1)} custom-call(bf16[2,256,1536]{2,1,0:T(8,128)(2,1)S(1)} %copy-done, f32[1,1536]{1,0:T(1,128)S(1)} %reshape.6.vit_gain, bf16[384,768]{1,0:T(8,128)(2,1)S(1)} %copy-done.1, bf16[384,768]{1,0:T(8,128)(2,1)S(1)} %copy-done.2, bf16[384,768]{1,0:T(8,128)(2,1)S(1)} %copy-done.3, bf16[192,1536]{1,0:T(8,128)(2,1)S(1)} %copy-done.4, ...), custom_call_target="tpu_custom_call" | custom-call | flops 305135616 | bytes 8388608 | tf_op jit(solution)/shard_map/pallas_call | solution.py:318
  47.2 0.6 %copy.20 = bf16[8,192]{1,0:T(8,128)(2,1)} copy(bf16[8,192]{1,0:T(8,128)(2,1)S(1)} %shard_map.136) | data formatting | bytes 6144
Async XLA Ops:
  0.0 5.6 %copy-start.7 = (s32[2]{0:T(128)S(1)}, s32[2]{0:T(128)}, u32[]{:S(2)}) copy-start(s32[2]{0:T(128)} %order.1) | copy-start | bytes 28
  0.0 5.6 %copy-start.6 = (bf16[192,768]{1,0:T(8,128)(2,1)S(1)}, bf16[192,768]{1,0:T(8,128)(2,1)}, u32[]{:S(2)}) copy-start(bf16[192,768]{1,0:T(8,128)(2,1)} %long_out.1) | copy-start | bytes 884740
  0.0 5.6 %copy-start = (bf16[2,256,1536]{2,1,0:T(8,128)(2,1)S(1)}, bf16[2,256,1536]{2,1,0:T(8,128)(2,1)}, u32[]{:S(2)}) copy-start(bf16[2,256,1536]{2,1,0:T(8,128)(2,1)} %patches.1) | copy-start | bytes 4718596
  5.6 1.1 %copy-start.1 = (bf16[384,768]{1,0:T(8,128)(2,1)S(1)}, bf16[384,768]{1,0:T(8,128)(2,1)}, u32[]{:S(2)}) copy-start(bf16[384,768]{1,0:T(8,128)(2,1)} %w_query.1) | copy-start | bytes 1769476
  6.7 1.1 %copy-start.2 = (bf16[384,768]{1,0:T(8,128)(2,1)S(1)}, bf16[384,768]{1,0:T(8,128)(2,1)}, u32[]{:S(2)}) copy-start(bf16[384,768]{1,0:T(8,128)(2,1)} %w_key.1) | copy-start | bytes 1769476
  7.8 1.1 %copy-start.3 = (bf16[384,768]{1,0:T(8,128)(2,1)S(1)}, bf16[384,768]{1,0:T(8,128)(2,1)}, u32[]{:S(2)}) copy-start(bf16[384,768]{1,0:T(8,128)(2,1)} %w_value.1) | copy-start | bytes 1769476
  8.8 1.1 %copy-start.4 = (bf16[192,1536]{1,0:T(8,128)(2,1)S(1)}, bf16[192,1536]{1,0:T(8,128)(2,1)}, u32[]{:S(2)}) copy-start(bf16[192,1536]{1,0:T(8,128)(2,1)} %w_out.1) | copy-start | bytes 1769476
  9.9 1.1 %copy-start.5 = (bf16[384,768]{1,0:T(8,128)(2,1)S(1)}, bf16[384,768]{1,0:T(8,128)(2,1)}, u32[]{:S(2)}) copy-start(bf16[384,768]{1,0:T(8,128)(2,1)} %w_proj.1) | copy-start | bytes 1769476

commit v2 on v1

--- a/solution.py
+++ b/solution.py
@@ -12,10 +12,20 @@
 HEADS = 16
 DILATION_STEP = 4
 EPSILON = 1e-06
-LN_ROWS = 32
+LN_ROWS = 64
 
 F32 = jnp.float32
 BF16 = jnp.bfloat16
+
+
+def stack_halves(x):
+    half = x.shape[1] // 2
+    return jnp.concatenate([x[:, :half], x[:, half:]], axis=0)
+
+
+def join_halves(x):
+    half = x.shape[0] // 2
+    return jnp.concatenate([x[:half], x[half:]], axis=1)
 
 
 def up(n, m):
@@ -40,8 +50,8 @@
 def kernel(
     F, S,
     patches, vit_gain, w_query, w_key, w_value, w_out, w_proj,
-    long_gain, long_query, long_key, long_value, long_out, order, counts,
-    out,
+    long_gain, long_query, long_key, long_value, long_out, order_hbm, counts,
+    out, order,
     cls, xbuf, normed, wq, wk, wv, wo, wp, lq, lk, lv, lo,
     s1, r1, sm, rm, sm2, rm2, s2, r2, s3, r3, s4, r4, s5, r5, s6, r6, s7, r7,
     s8, r8, s9, r9, qbuf, seqc,
@@ -53,7 +63,7 @@
     R = T * F
     N = R * S
     C = DV // F
-    HC = long_query.shape[1]
+    HC = long_query.shape[0]
     OC = D // F
     PC = VW // F
     HP = up(VW // VHD, 16)
@@ -78,6 +88,7 @@
         pl.semaphore_signal(
             barrier, inc=1, device_id={"seq": lax.rem(z + k, S)},
             device_id_type=pl.DeviceIdType.MESH)
+    ld_order = load(order_hbm, order)
     ld_wq = load(w_query, wq)
     ld_x = [load(patches.at[t], xbuf.at[t]) for t in range(T)]
     ld_wk = load(w_key, wk)
@@ -129,11 +140,23 @@
         collect(hop, "seq", z, S, dst, zsend, zrecv)
 
     def total(ref, n):
-        acc = ref[0]
+        part = lambda j: ref[j].astype(F32) if ref.dtype == BF16 else ref[j]
+        acc = part(0)
         for j in range(1, n):
-            acc = acc + ref[j]
+            acc = acc + part(j)
         return acc
 
+    ld_cls.wait()
+    raw = jnp.concatenate([cls[t, 0:8, :].astype(F32)[0:1] for t in range(T)], axis=0)
+    class_normed = norm_rows(raw, vit_gain[...].reshape(1, DV)).astype(BF16).astype(F32)
+    filler = s1.shape[1] - 2 * T
+    packed = jnp.concatenate(
+        [class_normed, raw, jnp.zeros((filler, DV), F32)], axis=0)
+    for j in range(F):
+        s1[j] = packed[:, j * C:(j + 1) * C]
+    pl.semaphore_wait(barrier, F - 1 + S - 1)
+    scatter(0, s1, r1)
+    ld_order.wait()
     L = sm.shape[1]
     lane = lax.broadcasted_iota(jnp.int32, sm.shape, 1)
     row = lax.broadcasted_iota(jnp.int32, sm.shape, 0)
@@ -144,17 +167,6 @@
         value = jnp.where(row == 0, order[t] + 1, jnp.where(row == 1, here, 0))
         meta = jnp.where(lane == first + t, value, meta)
     sm[...] = meta
-
-    ld_cls.wait()
-    raw = jnp.concatenate([cls[t, 0:8, :].astype(F32)[0:1] for t in range(T)], axis=0)
-    class_normed = norm_rows(raw, vit_gain[...]).astype(BF16).astype(F32)
-    filler = s1.shape[1] - 2 * T
-    packed = jnp.concatenate(
-        [class_normed, raw, jnp.zeros((filler, DV), F32)], axis=0)
-    for j in range(F):
-        s1[j] = packed[:, j * C:(j + 1) * C]
-    pl.semaphore_wait(barrier, F - 1 + S - 1)
-    scatter(0, s1, r1)
     spread(1, sm, rm)
 
     blocks = PATCH // LN_ROWS
@@ -164,7 +176,7 @@
             t = i // blocks
             start = pl.multiple_of((i % blocks) * LN_ROWS, LN_ROWS)
             x = xbuf[t, pl.ds(start, LN_ROWS), :].astype(F32)
-            y = norm_rows(x, vit_gain[...])
+            y = norm_rows(x, vit_gain[...].reshape(1, DV))
             for j in range(F):
                 normed[t, j, pl.ds(start, LN_ROWS), :] = y[:, j * C:(j + 1) * C].astype(BF16)
             return carry
@@ -178,7 +190,7 @@
     ld_wq.wait()
     arrive(0, r1)
     xq = jnp.concatenate([r1[j][0:T] for j in range(F)], axis=0)
-    s2[...] = dot(xq.astype(BF16), wq[...])
+    s2[...] = stack_halves(dot(xq.astype(BF16), wq[...])).astype(BF16)
     spread(2, s2, r2)
     arrive(1, rm)
     sm2[...] = total(rm, F)
@@ -186,7 +198,7 @@
     norm_blocks(third, 2 * third)
     ld_wk.wait()
     arrive(2, r2)
-    query = total(r2, F).astype(BF16).astype(F32)
+    query = join_halves(total(r2, F).astype(BF16).astype(F32))
 
     head = lax.broadcasted_iota(jnp.int32, (R, HP, VW), 1)
     column = lax.broadcasted_iota(jnp.int32, (R, HP, VW), 2)
@@ -226,7 +238,7 @@
     ld_wp.wait()
     arrive(6, r6)
     class_row = (class_raw + total(r6, F)).astype(BF16)
-    s7[...] = dot(class_row, wp[...])
+    s7[...] = stack_halves(dot(class_row, wp[...])).astype(BF16)
     spread(7, s7, r7)
 
     arrive_z(0, rm2)
@@ -239,9 +251,7 @@
     key_present = dot_t(jnp.broadcast_to(all_present, (8, N)).astype(BF16), picker.astype(BF16))[0:1]
 
     arrive(7, r7)
-    embeds = total(r7, F).astype(BF16).astype(F32)
-    half = D // 2
-    s8[...] = jnp.concatenate([embeds[:, :half], embeds[:, half:]], axis=0).astype(BF16)
+    s8[...] = total(r7, F).astype(BF16)
     spread_z(1, s8, r8)
     heads_dev = HC // (D // HEADS)
     hw = D // HEADS
@@ -270,10 +280,10 @@
     right = jnp.concatenate([r8[j].astype(F32)[R:] for j in range(S)], axis=0)
     every = jnp.concatenate([left, right], axis=1).astype(BF16)
     sequence = dot(picker_tissue, every)
-    lnormed = norm_rows(sequence, long_gain[...]).astype(BF16)
-    qbuf[...] = dot(lnormed, lq[...])
-    keys = dot(lnormed, lk[...]).astype(BF16)
-    values = dot(lnormed, lv[...]).astype(BF16)
+    lnormed = norm_rows(sequence, long_gain[...].reshape(1, D)).astype(BF16)
+    qbuf[...] = dot_t(lnormed, lq[...])
+    keys = dot_t(lnormed, lk[...]).astype(BF16)
+    values = dot_t(lnormed, lv[...]).astype(BF16)
     queries = qbuf[pl.ds(pl.multiple_of(z * R, R), R), :].astype(BF16).astype(F32)
     per_head = jnp.where(mine, queries[None], 0.0).reshape(heads_dev * R, HC).astype(BF16)
     lifted = jnp.exp(dot_t(per_head, keys) / math.sqrt(hw))
@@ -299,18 +309,18 @@
     tile_patches, vit_gain, w_query, w_key, w_value, w_out, w_proj,
     long_gain, long_query, long_key, long_value, long_out, seq_order, counts,
 ):
+    long_query, long_key, long_value = long_query.T, long_key.T, long_value.T
     S = lax.axis_size("seq")
     F = lax.axis_size("fsdp")
     T, PATCH, DV = tile_patches.shape
     VW = w_key.shape[1]
     D = w_proj.shape[1]
-    R, C, HC, OC, PC = T * F, DV // F, long_query.shape[1], D // F, VW // F
+    R, C, HC, OC, PC = T * F, DV // F, long_query.shape[0], D // F, VW // F
     HP = up(VW // VHD, 16)
     N = R * S
     L = up(N, 128)
     V = pltpu.VMEM
-    any_, vmem, smem = (
-        pl.BlockSpec(memory_space=m) for m in (pl.ANY, pltpu.VMEM, pltpu.SMEM))
+    any_, vmem = pl.BlockSpec(memory_space=pl.ANY), pl.BlockSpec(memory_space=pltpu.VMEM)
     like = lambda a: V(a.shape, a.dtype)
     pair = lambda shape, dtype: [V((F,) + shape, dtype), V((F,) + shape, dtype)]
     fan = lambda n, shape, dtype: [V(shape, dtype), V((n,) + shape, dtype)]
@@ -319,35 +329,36 @@
         functools.partial(kernel, F, S),
         out_shape=jax.ShapeDtypeStruct((R, OC), BF16),
         in_specs=[any_, vmem, any_, any_, any_, any_, any_, vmem,
-                  any_, any_, any_, any_, smem, smem],
+                  any_, any_, any_, any_, any_, pl.BlockSpec(memory_space=pltpu.SMEM)],
         out_specs=vmem,
         scratch_shapes=[
+            pltpu.SMEM(seq_order.shape, jnp.int32),
             V((T, 16, DV), BF16), like(tile_patches), V((T, F, PATCH, C), BF16),
             like(w_query), like(w_key), like(w_value), like(w_out), like(w_proj),
             like(long_query), like(long_key), like(long_value), like(long_out),
             *pair((up(2 * T, 8), C), F32),
             *fan(F, (8, L), jnp.int32),
             *fan(S, (8, L), jnp.int32),
-            *fan(F, (R, VW), F32),
+            *fan(F, (2 * R, VW // 2), BF16),
             *pair((T * HP, C), BF16),
             *pair((T * HP, C), BF16),
             *pair((R, PC), F32),
             *pair((R, C), F32),
-            *fan(F, (R, D), F32),
+            *fan(F, (2 * R, D // 2), BF16),
             *fan(S, (2 * R, D // 2), BF16),
             *pair((R, OC), F32),
             V((N, HC), F32), V((F, N, OC), F32),
-            pltpu.SemaphoreType.DMA((10 + T,)),
+            pltpu.SemaphoreType.DMA((11 + T,)),
             pltpu.SemaphoreType.DMA((9, F)), pltpu.SemaphoreType.DMA((9, F)),
             pltpu.SemaphoreType.DMA((2, S)), pltpu.SemaphoreType.DMA((2, S)),
         ],
         compiler_params=pltpu.CompilerParams(
-            collective_id=0, has_side_effects=True, vmem_limit_bytes=48 * 2**20),
+            collective_id=0, has_side_effects=True, vmem_limit_bytes=60 * 2**20),
         cost_estimate=pl.CostEstimate(
             flops=flops, bytes_accessed=8 * 2**20, transcendentals=T * HP * PATCH),
     )(
-        tile_patches, vit_gain.reshape(1, DV), w_query, w_key, w_value, w_out, w_proj,
-        long_gain.reshape(1, D), long_query, long_key, long_value, long_out,
+        tile_patches, vit_gain, w_query, w_key, w_value, w_out, w_proj,
+        long_gain, long_query, long_key, long_value, long_out,
         seq_order, counts,
     )
 

time: 48.3 us -> 38.5 us (0.80)
  local copies, waits for them, and re-layouts: 10.7 us -> 1.28 us
    unnamed x20 -> x1, local copies, waits for them, and re-layouts: 9.31 us -> 1.28 us
    reshape x2 -> x0, local copies, waits for them, and re-layouts: 1.39 us -> none  [the longest x1 0.7 us: local(): vit_gain.reshape(1, DV)]
where the time goes in v2:
time: 38.5 us; the launch traced here: 38.3 us
  Pallas kernels  36.3 us (94%)
  local copies, waits for them, and re-layouts  1.28 us (3%)
  between operations  0.66 us (2%)
    pallas_call x1, Pallas kernels, local(): pl.pallas_call(functools.partial(kernel, F, S), out_shape=jax.ShapeDtypeS...  36.3 us
    unnamed x1, local copies, waits for them, and re-layouts  1.28 us

profile of v2, /device:TPU:0, one launch (start us, length us, event | category | flops | bytes accessed | tf_op | source)
XLA Modules:
  0.0 38.3 jit_solution(335540489779283364)
XLA Ops:
  0.7 36.3 %shard_map.136 = bf16[8,192]{1,0:T(8,128)(2,1)} custom-call(bf16[2,256,1536]{2,1,0:T(8,128)(2,1)} %patches.1, f32[1536]{0:T(1024)} %vit_gain.1, bf16[384,768]{1,0:T(8,128)(2,1)} %w_query.1, bf16[384,768]{1,0:T(8,128)(2,1)} %w_key.1, bf16[384,768]{1,0:T(8,128)(2,1)} %w_value.1, bf16[192,1536]{1,0:T(8,128)(2,1)} %w_out.1, bf16[384,768]{1,0:T(8,128)(2,1)} %w_proj.1, ...), custom_call_target="tpu_custom_call" | custom-call | flops 305135616 | bytes 8388608 | tf_op jit(solution)/shard_map/pallas_call | solution.py:328
  37.0 1.3 %copy.17 = bf16[8,192]{1,0:T(8,128)(2,1)} copy(bf16[8,192]{1,0:T(8,128)(2,1)} %shard_map.136) | data formatting | bytes 6144

commit v3 on v2

--- a/solution.py
+++ b/solution.py
@@ -49,9 +49,9 @@
 
 def kernel(
     F, S,
-    patches, vit_gain, w_query, w_key, w_value, w_out, w_proj,
-    long_gain, long_query, long_key, long_value, long_out, order_hbm, counts,
-    out, order,
+    patches, vit_gain_hbm, w_query, w_key, w_value, w_out, w_proj,
+    long_gain_hbm, long_query, long_key, long_value, long_out, order_hbm, counts,
+    out, order, vit_gain, long_gain,
     cls, xbuf, normed, wq, wk, wv, wo, wp, lq, lk, lv, lo,
     s1, r1, sm, rm, sm2, rm2, s2, r2, s3, r3, s4, r4, s5, r5, s6, r6, s7, r7,
     s8, r8, s9, r9, qbuf, seqc,
@@ -79,6 +79,7 @@
         return c
 
     ld_cls = load(patches.at[:, pl.ds(0, 16), :], cls)
+    ld_vg = load(vit_gain_hbm, vit_gain)
     barrier = pltpu.get_barrier_semaphore()
     for k in range(1, F):
         pl.semaphore_signal(
@@ -95,6 +96,7 @@
     ld_wv = load(w_value, wv)
     ld_wo = load(w_out, wo)
     ld_wp = load(w_proj, wp)
+    ld_lg = load(long_gain_hbm, long_gain)
     ld_lq = load(long_query, lq)
     ld_lk = load(long_key, lk)
     ld_lv = load(long_value, lv)
@@ -147,6 +149,7 @@
         return acc
 
     ld_cls.wait()
+    ld_vg.wait()
     raw = jnp.concatenate([cls[t, 0:8, :].astype(F32)[0:1] for t in range(T)], axis=0)
     class_normed = norm_rows(raw, vit_gain[...].reshape(1, DV)).astype(BF16).astype(F32)
     filler = s1.shape[1] - 2 * T
@@ -182,10 +185,10 @@
             return carry
         lax.fori_loop(lo_block, hi_block, body, 0)
 
-    third = T * blocks // 3
+    cuts = (3 * T * blocks // 8, 5 * T * blocks // 8)
     for c in ld_x:
         c.wait()
-    norm_blocks(0, third)
+    norm_blocks(0, cuts[0])
 
     ld_wq.wait()
     arrive(0, r1)
@@ -195,19 +198,19 @@
     arrive(1, rm)
     sm2[...] = total(rm, F)
     spread_z(0, sm2, rm2)
-    norm_blocks(third, 2 * third)
+    norm_blocks(*cuts)
+    head = lax.broadcasted_iota(jnp.int32, (R, HP, VW), 1)
+    column = lax.broadcasted_iota(jnp.int32, (R, HP, VW), 2)
+    own_head = (column >= head * VHD) & (column < (head + 1) * VHD)
     ld_wk.wait()
     arrive(2, r2)
     query = join_halves(total(r2, F).astype(BF16).astype(F32))
 
-    head = lax.broadcasted_iota(jnp.int32, (R, HP, VW), 1)
-    column = lax.broadcasted_iota(jnp.int32, (R, HP, VW), 2)
-    own_head = (column >= head * VHD) & (column < (head + 1) * VHD)
     spread_query = jnp.where(own_head, query[:, None, :], 0.0).reshape(R * HP, VW)
     folded = dot_t(spread_query.astype(BF16), wk[...]).astype(BF16)
     s3[...] = folded.reshape(F, T * HP, C)
     scatter(3, s3, r3)
-    norm_blocks(2 * third, T * blocks)
+    norm_blocks(cuts[1], T * blocks)
     arrive(3, r3)
 
     for t in range(T):
@@ -228,6 +231,20 @@
     for j in range(F):
         s5[j] = pooled_part[:, j * PC:(j + 1) * PC]
     scatter(5, s5, r5)
+    heads_dev = HC // (D // HEADS)
+    hw = D // HEADS
+    hr = (heads_dev, R, N)
+    m_head = lax.broadcasted_iota(jnp.int32, hr, 0) + f * heads_dev
+    m_row = lax.broadcasted_iota(jnp.int32, hr, 1) + z * R
+    m_key = lax.broadcasted_iota(jnp.int32, hr, 2)
+    segment = N // 4
+    in_local = m_row // segment == m_key // segment
+    in_dilated = (m_row % DILATION_STEP == m_head % DILATION_STEP) & (
+        m_key % DILATION_STEP == m_head % DILATION_STEP)
+    sets = jnp.where(in_local, 1.0, 0.0) + jnp.where(in_dilated, 1.0, 0.0)
+    a_head = lax.broadcasted_iota(jnp.int32, (heads_dev, R, HC), 0)
+    a_col = lax.broadcasted_iota(jnp.int32, (heads_dev, R, HC), 2)
+    mine = (a_col >= a_head * hw) & (a_col < (a_head + 1) * hw)
     arrive(5, r5)
     pooled = total(r5, F).astype(BF16)
     row_part = dot(pooled, wo[...])
@@ -250,26 +267,12 @@
     picker_tissue = (picker * all_present).astype(BF16)
     key_present = dot_t(jnp.broadcast_to(all_present, (8, N)).astype(BF16), picker.astype(BF16))[0:1]
 
+    allowed = (key_present.reshape(1, 1, N) > 0.5) | (m_row == m_key)
+    times = jnp.where(allowed, sets, 0.0).reshape(heads_dev * R, N)
     arrive(7, r7)
     s8[...] = total(r7, F).astype(BF16)
     spread_z(1, s8, r8)
-    heads_dev = HC // (D // HEADS)
-    hw = D // HEADS
-    hr = (heads_dev, R, N)
-    m_head = lax.broadcasted_iota(jnp.int32, hr, 0) + f * heads_dev
-    m_row = lax.broadcasted_iota(jnp.int32, hr, 1) + z * R
-    m_key = lax.broadcasted_iota(jnp.int32, hr, 2)
-    segment = N // 4
-    allowed = (key_present.reshape(1, 1, N) > 0.5) | (m_row == m_key)
-    in_local = m_row // segment == m_key // segment
-    in_dilated = (m_row % DILATION_STEP == m_head % DILATION_STEP) & (
-        m_key % DILATION_STEP == m_head % DILATION_STEP)
-    times = jnp.where(
-        allowed, jnp.where(in_local, 1.0, 0.0) + jnp.where(in_dilated, 1.0, 0.0), 0.0
-    ).reshape(heads_dev * R, N)
-    a_head = lax.broadcasted_iota(jnp.int32, (heads_dev, R, HC), 0)
-    a_col = lax.broadcasted_iota(jnp.int32, (heads_dev, R, HC), 2)
-    mine = (a_col >= a_head * hw) & (a_col < (a_head + 1) * hw)
+    ld_lg.wait()
     ld_lq.wait()
     ld_lk.wait()
     ld_lv.wait()
@@ -327,12 +330,12 @@
     flops = 2 * (3 * R * HP * C * VW + 2 * T * HP * PATCH * DV + 3 * N * D * HC)
     return pl.pallas_call(
         functools.partial(kernel, F, S),
-        out_shape=jax.ShapeDtypeStruct((R, OC), BF16),
-        in_specs=[any_, vmem, any_, any_, any_, any_, any_, vmem,
+        out_shape=pltpu.VMEM((R, OC), BF16),
+        in_specs=[any_, any_, any_, any_, any_, any_, any_, any_,
                   any_, any_, any_, any_, any_, pl.BlockSpec(memory_space=pltpu.SMEM)],
         out_specs=vmem,
         scratch_shapes=[
-            pltpu.SMEM(seq_order.shape, jnp.int32),
+            pltpu.SMEM(seq_order.shape, jnp.int32), like(vit_gain), like(long_gain),
             V((T, 16, DV), BF16), like(tile_patches), V((T, F, PATCH, C), BF16),
             like(w_query), like(w_key), like(w_value), like(w_out), like(w_proj),
             like(long_query), like(long_key), like(long_value), like(long_out),
@@ -348,7 +351,7 @@
             *fan(S, (2 * R, D // 2), BF16),
             *pair((R, OC), F32),
             V((N, HC), F32), V((F, N, OC), F32),
-            pltpu.SemaphoreType.DMA((11 + T,)),
+            pltpu.SemaphoreType.DMA((13 + T,)),
             pltpu.SemaphoreType.DMA((9, F)), pltpu.SemaphoreType.DMA((9, F)),
             pltpu.SemaphoreType.DMA((2, S)), pltpu.SemaphoreType.DMA((2, S)),
         ],

time: 38.5 us -> 36.5 us (0.948)
  Pallas kernels: 36.3 us -> 35.1 us
  local copies, waits for them, and re-layouts: 1.28 us -> 0.6 us
    pallas_call x1, Pallas kernels: 36.3 us -> 35.1 us  [local(): pl.pallas_call(functools.partial(kernel, F, S), out_shape=pltpu.VMEM((R,...]
    unnamed x1, local copies, waits for them, and re-layouts: 1.28 us -> 0.6 us
where the time goes in v3:
time: 36.5 us; the launch traced here: 36.3 us
  Pallas kernels  35.1 us (96%)
  between operations  0.66 us (2%)
  local copies, waits for them, and re-layouts  0.6 us (2%)
    pallas_call x1, Pallas kernels, local(): pl.pallas_call(functools.partial(kernel, F, S), out_shape=pltpu.VMEM((R,...  35.1 us

profile of v3, /device:TPU:0, one launch (start us, length us, event | category | flops | bytes accessed | tf_op | source)
XLA Modules:
  0.0 36.3 jit_solution(15325061119173625870)
XLA Ops:
  0.7 35.1 %shard_map.136 = bf16[8,192]{1,0:T(8,128)(2,1)S(1)} custom-call(bf16[2,256,1536]{2,1,0:T(8,128)(2,1)} %patches.1, f32[1536]{0:T(1024)} %vit_gain_hbm.1, bf16[384,768]{1,0:T(8,128)(2,1)} %w_query.1, bf16[384,768]{1,0:T(8,128)(2,1)} %w_key.1, bf16[384,768]{1,0:T(8,128)(2,1)} %w_value.1, bf16[192,1536]{1,0:T(8,128)(2,1)} %w_out.1, bf16[384,768]{1,0:T(8,128)(2,1)} %w_proj.1, ...), custom_call_target="tpu_custom_call" | custom-call | flops 305135616 | bytes 8388608 | tf_op jit(solution)/shard_map/pallas_call | solution.py:331
  35.7 0.6 %copy.16 = bf16[8,192]{1,0:T(8,128)(2,1)} copy(bf16[8,192]{1,0:T(8,128)(2,1)S(1)} %shard_map.136) | data formatting | bytes 6144

commit v4 on v3

--- a/solution.py
+++ b/solution.py
@@ -214,9 +214,10 @@
     arrive(3, r3)
 
     for t in range(T):
-        scores = dot_t(r3[0, pl.ds(t * HP, HP), :], normed[t, 0])
+        by_token = dot_t(normed[t, 0], r3[0])
         for j in range(1, F):
-            scores = scores + dot_t(r3[j, pl.ds(t * HP, HP), :], normed[t, j])
+            by_token = by_token + dot_t(normed[t, j], r3[j])
+        scores = jnp.transpose(by_token)[t * HP:(t + 1) * HP]
         lifted = jnp.exp(scores / math.sqrt(VHD))
         probs = (lifted / jnp.sum(lifted, axis=-1, keepdims=True)).astype(BF16)
         for j in range(F):
@@ -302,9 +303,11 @@
     for j in range(F):
         seqc[j] = sequence[:, j * OC:(j + 1) * OC]
     residual = seqc[f, pl.ds(pl.multiple_of(z * R, R), R), :]
+    for c in sends[:1 - F]:
+        c.wait_send()
     arrive(8, r9)
     out[...] = (residual + total(r9, F)).astype(BF16)
-    for c in sends:
+    for c in sends[1 - F:]:
         c.wait_send()
 
 

time: 36.5 us -> 36.1 us (0.989)
  Pallas kernels: 35.1 us -> 34.7 us
    pallas_call x1, Pallas kernels: 35.1 us -> 34.7 us  [local(): pl.pallas_call(functools.partial(kernel, F, S), out_shape=pltpu.VMEM((R,...]
where the time goes in v4:
time: 36.1 us; the launch traced here: 36 us
  Pallas kernels  34.7 us (96%)
  between operations  0.66 us (2%)
  local copies, waits for them, and re-layouts  0.6 us (2%)
    pallas_call x1, Pallas kernels, local(): pl.pallas_call(functools.partial(kernel, F, S), out_shape=pltpu.VMEM((R,...  34.7 us

profile of v4, /device:TPU:0, one launch (start us, length us, event | category | flops | bytes accessed | tf_op | source)
XLA Modules:
  0.0 36.0 jit_solution(18053071654887352991)
XLA Ops:
  0.7 34.7 %shard_map.136 = bf16[8,192]{1,0:T(8,128)(2,1)S(1)} custom-call(bf16[2,256,1536]{2,1,0:T(8,128)(2,1)} %patches.1, f32[1536]{0:T(1024)} %vit_gain_hbm.1, bf16[384,768]{1,0:T(8,128)(2,1)} %w_query.1, bf16[384,768]{1,0:T(8,128)(2,1)} %w_key.1, bf16[384,768]{1,0:T(8,128)(2,1)} %w_value.1, bf16[192,1536]{1,0:T(8,128)(2,1)} %w_out.1, bf16[384,768]{1,0:T(8,128)(2,1)} %w_proj.1, ...), custom_call_target="tpu_custom_call" | custom-call | flops 305135616 | bytes 8388608 | tf_op jit(solution)/shard_map/pallas_call | solution.py:334
  35.4 0.6 %copy.16 = bf16[8,192]{1,0:T(8,128)(2,1)} copy(bf16[8,192]{1,0:T(8,128)(2,1)S(1)} %shard_map.136) | data formatting | bytes 6144

commit v5 on v4

--- a/solution.py
+++ b/solution.py
@@ -32,6 +32,17 @@
     return (n + m - 1) // m * m
 
 
+def partners(me, n):
+    if n % 2:
+        return [lax.rem(me + k, n) for k in range(1, n)]
+    pair, side = me // 2, me % 2
+    found = []
+    for k in range(1, n // 2):
+        other = lax.rem(pair + k, n // 2) * 2
+        found += [other + side, other + 1 - side]
+    return found + [pair * 2 + 1 - side]
+
+
 def norm_rows(x, gain):
     mean = jnp.mean(x, axis=-1, keepdims=True)
     centred = x - mean
@@ -52,7 +63,7 @@
     patches, vit_gain_hbm, w_query, w_key, w_value, w_out, w_proj,
     long_gain_hbm, long_query, long_key, long_value, long_out, order_hbm, counts,
     out, order, vit_gain, long_gain,
-    cls, xbuf, normed, wq, wk, wv, wo, wp, lq, lk, lv, lo,
+    cls, xbuf, normed, wq, wk, wv, wo, wp, lqkv, lo,
     s1, r1, sm, rm, sm2, rm2, s2, r2, s3, r3, s4, r4, s5, r5, s6, r6, s7, r7,
     s8, r8, s9, r9, qbuf, seqc,
     lsem, fsend, frecv, zsend, zrecv,
@@ -97,16 +108,15 @@
     ld_wo = load(w_out, wo)
     ld_wp = load(w_proj, wp)
     ld_lg = load(long_gain_hbm, long_gain)
-    ld_lq = load(long_query, lq)
-    ld_lk = load(long_key, lk)
-    ld_lv = load(long_value, lv)
+    ld_lq = load(long_query, lqkv.at[0])
+    ld_lk = load(long_key, lqkv.at[1])
+    ld_lv = load(long_value, lqkv.at[2])
     ld_lo = load(long_out, lo)
 
     sends = []
 
     def push(hop, axis, me, n, src, dst, send_sems, recv_sems):
-        for k in sorted(range(1, n), key=lambda k: abs(2 * k - n)):
-            peer = lax.rem(me + k, n)
+        for k, peer in enumerate(partners(me, n)):
             c = pltpu.make_async_remote_copy(
                 src_ref=src(peer), dst_ref=dst.at[me],
                 send_sem=send_sems.at[hop, k], recv_sem=recv_sems.at[hop, me],
@@ -115,8 +125,7 @@
             sends.append(c)
 
     def collect(hop, axis, me, n, dst, send_sems, recv_sems):
-        for k in range(1, n):
-            peer = lax.rem(me + k, n)
+        for k, peer in enumerate(reversed(partners(me, n))):
             pltpu.make_async_remote_copy(
                 src_ref=dst.at[me], dst_ref=dst.at[peer],
                 send_sem=send_sems.at[hop, k], recv_sem=recv_sems.at[hop, peer],
@@ -169,9 +178,14 @@
         here = jnp.where(t < counts[0], 1, 0)
         value = jnp.where(row == 0, order[t] + 1, jnp.where(row == 1, here, 0))
         meta = jnp.where(lane == first + t, value, meta)
+        split = 2 * z * R + f * T + t + jnp.where(row == 3, R, 0)
+        meta = jnp.where(
+            (row >= 2) & (row < 4) & (lane == split), jnp.where(t < counts[0], order[t] + 1, 0), meta)
     sm[...] = meta
     spread(1, sm, rm)
 
+    s5[...] = jnp.zeros(s5.shape, F32)
+    s9[...] = jnp.zeros(s9.shape, F32)
     blocks = PATCH // LN_ROWS
 
     def norm_blocks(lo_block, hi_block):
@@ -230,7 +244,7 @@
     summed = dot(r4[...].reshape(R * HP, C), wv[...]).reshape(R, HP, VW)
     pooled_part = jnp.sum(jnp.where(own_head, summed, 0.0), axis=1)
     for j in range(F):
-        s5[j] = pooled_part[:, j * PC:(j + 1) * PC]
+        s5[j, :, 0:PC] = pooled_part[:, j * PC:(j + 1) * PC]
     scatter(5, s5, r5)
     heads_dev = HC // (D // HEADS)
     hw = D // HEADS
@@ -247,7 +261,7 @@
     a_col = lax.broadcasted_iota(jnp.int32, (heads_dev, R, HC), 2)
     mine = (a_col >= a_head * hw) & (a_col < (a_head + 1) * hw)
     arrive(5, r5)
-    pooled = total(r5, F).astype(BF16)
+    pooled = total(r5, F)[:, :PC].astype(BF16)
     row_part = dot(pooled, wo[...])
     for j in range(F):
         s6[j] = row_part[:, j * C:(j + 1) * C]
@@ -265,7 +279,9 @@
     all_present = all_meta[1:2, 0:N].astype(F32)
     position = lax.broadcasted_iota(jnp.int32, (N, N), 0) + 1
     picker = jnp.where(position == all_order, 1.0, 0.0)
-    picker_tissue = (picker * all_present).astype(BF16)
+    place = lax.broadcasted_iota(jnp.int32, (N, 2 * N), 0) + 1
+    pick_left = jnp.where(place == all_meta[2:3, 0:2 * N], 1.0, 0.0).astype(BF16)
+    pick_right = jnp.where(place == all_meta[3:4, 0:2 * N], 1.0, 0.0).astype(BF16)
     key_present = dot_t(jnp.broadcast_to(all_present, (8, N)).astype(BF16), picker.astype(BF16))[0:1]
 
     allowed = (key_present.reshape(1, 1, N) > 0.5) | (m_row == m_key)
@@ -280,14 +296,13 @@
     ld_lo.wait()
     arrive_z(1, r8)
 
-    left = jnp.concatenate([r8[j].astype(F32)[:R] for j in range(S)], axis=0)
-    right = jnp.concatenate([r8[j].astype(F32)[R:] for j in range(S)], axis=0)
-    every = jnp.concatenate([left, right], axis=1).astype(BF16)
-    sequence = dot(picker_tissue, every)
+    every = r8[...].reshape(2 * N, D // 2)
+    sequence = jnp.concatenate([dot(pick_left, every), dot(pick_right, every)], axis=1)
     lnormed = norm_rows(sequence, long_gain[...].reshape(1, D)).astype(BF16)
-    qbuf[...] = dot_t(lnormed, lq[...])
-    keys = dot_t(lnormed, lk[...]).astype(BF16)
-    values = dot_t(lnormed, lv[...]).astype(BF16)
+    projected = dot_t(lnormed, lqkv[...].reshape(3 * HC, D))
+    qbuf[...] = projected[:, :HC]
+    keys = projected[:, HC:2 * HC].astype(BF16)
+    values = projected[:, 2 * HC:].astype(BF16)
     queries = qbuf[pl.ds(pl.multiple_of(z * R, R), R), :].astype(BF16).astype(F32)
     per_head = jnp.where(mine, queries[None], 0.0).reshape(heads_dev * R, HC).astype(BF16)
     lifted = jnp.exp(dot_t(per_head, keys) / math.sqrt(hw))
@@ -298,7 +313,7 @@
         jnp.where(mine, mixed.reshape(heads_dev, R, HC), 0.0), axis=0).astype(BF16)
     terms = dot(attended, lo[...])
     for j in range(F):
-        s9[j] = terms[:, j * OC:(j + 1) * OC]
+        s9[j, :, 0:OC] = terms[:, j * OC:(j + 1) * OC]
     scatter(8, s9, r9)
     for j in range(F):
         seqc[j] = sequence[:, j * OC:(j + 1) * OC]
@@ -306,7 +321,7 @@
     for c in sends[:1 - F]:
         c.wait_send()
     arrive(8, r9)
-    out[...] = (residual + total(r9, F)).astype(BF16)
+    out[...] = (residual + total(r9, F)[:, :OC]).astype(BF16)
     for c in sends[1 - F:]:
         c.wait_send()
 
@@ -324,7 +339,7 @@
     R, C, HC, OC, PC = T * F, DV // F, long_query.shape[0], D // F, VW // F
     HP = up(VW // VHD, 16)
     N = R * S
-    L = up(N, 128)
+    L = up(2 * N, 128)
     V = pltpu.VMEM
     any_, vmem = pl.BlockSpec(memory_space=pl.ANY), pl.BlockSpec(memory_space=pltpu.VMEM)
     like = lambda a: V(a.shape, a.dtype)
@@ -341,18 +356,18 @@
             pltpu.SMEM(seq_order.shape, jnp.int32), like(vit_gain), like(long_gain),
             V((T, 16, DV), BF16), like(tile_patches), V((T, F, PATCH, C), BF16),
             like(w_query), like(w_key), like(w_value), like(w_out), like(w_proj),
-            like(long_query), like(long_key), like(long_value), like(long_out),
+            V((3,) + long_query.shape, BF16), like(long_out),
             *pair((up(2 * T, 8), C), F32),
             *fan(F, (8, L), jnp.int32),
             *fan(S, (8, L), jnp.int32),
             *fan(F, (2 * R, VW // 2), BF16),
             *pair((T * HP, C), BF16),
             *pair((T * HP, C), BF16),
-            *pair((R, PC), F32),
+            *pair((R, up(PC, 128)), F32),
             *pair((R, C), F32),
             *fan(F, (2 * R, D // 2), BF16),
             *fan(S, (2 * R, D // 2), BF16),
-            *pair((R, OC), F32),
+            *pair((R, up(OC, 128)), F32),
             V((N, HC), F32), V((F, N, OC), F32),
             pltpu.SemaphoreType.DMA((13 + T,)),
             pltpu.SemaphoreType.DMA((9, F)), pltpu.SemaphoreType.DMA((9, F)),

time: 36.1 us -> 36.2 us (level)
  no operation moved by 1% of the time
where the time goes in v5:
time: 36.2 us; the launch traced here: 36 us
  Pallas kernels  34.7 us (96%)
  between operations  0.66 us (2%)
  local copies, waits for them, and re-layouts  0.6 us (2%)
    pallas_call x1, Pallas kernels, local(): pl.pallas_call(functools.partial(kernel, F, S), out_shape=pltpu.VMEM((R,...  34.7 us

profile of v5, /device:TPU:0, one launch (start us, length us, event | category | flops | bytes accessed | tf_op | source)
XLA Modules:
  0.0 36.0 jit_solution(693975645816193556)
XLA Ops:
  0.7 34.7 %shard_map.136 = bf16[8,192]{1,0:T(8,128)(2,1)S(1)} custom-call(bf16[2,256,1536]{2,1,0:T(8,128)(2,1)} %patches.1, f32[1536]{0:T(1024)} %vit_gain_hbm.1, bf16[384,768]{1,0:T(8,128)(2,1)} %w_query.1, bf16[384,768]{1,0:T(8,128)(2,1)} %w_key.1, bf16[384,768]{1,0:T(8,128)(2,1)} %w_value.1, bf16[192,1536]{1,0:T(8,128)(2,1)} %w_out.1, bf16[384,768]{1,0:T(8,128)(2,1)} %w_proj.1, ...), custom_call_target="tpu_custom_call" | custom-call | flops 305135616 | bytes 8388608 | tf_op jit(solution)/shard_map/pallas_call | solution.py:349
  35.4 0.6 %copy.16 = bf16[8,192]{1,0:T(8,128)(2,1)} copy(bf16[8,192]{1,0:T(8,128)(2,1)S(1)} %shard_map.136) | data formatting | bytes 6144

commit v6 on v5

--- a/solution.py
+++ b/solution.py
@@ -12,7 +12,8 @@
 HEADS = 16
 DILATION_STEP = 4
 EPSILON = 1e-06
-LN_ROWS = 64
+LN_ROWS = 128
+LN_PART = 16
 
 F32 = jnp.float32
 BF16 = jnp.bfloat16
@@ -65,7 +66,7 @@
     out, order, vit_gain, long_gain,
     cls, xbuf, normed, wq, wk, wv, wo, wp, lqkv, lo,
     s1, r1, sm, rm, sm2, rm2, s2, r2, s3, r3, s4, r4, s5, r5, s6, r6, s7, r7,
-    s8, r8, s9, r9, qbuf, seqc,
+    s8, r8, s9, r9, qbuf, seqc, sumbuf,
     lsem, fsend, frecv, zsend, zrecv,
 ):
     T, PATCH, DV = patches.shape
@@ -188,18 +189,27 @@
     s9[...] = jnp.zeros(s9.shape, F32)
     blocks = PATCH // LN_ROWS
 
+    ones = jnp.full((DV, 128), 1.0, BF16)
+    gain_row = vit_gain[...].reshape(1, DV)
+
     def norm_blocks(lo_block, hi_block):
         def body(i, carry):
             t = i // blocks
-            start = pl.multiple_of((i % blocks) * LN_ROWS, LN_ROWS)
-            x = xbuf[t, pl.ds(start, LN_ROWS), :].astype(F32)
-            y = norm_rows(x, vit_gain[...].reshape(1, DV))
-            for j in range(F):
-                normed[t, j, pl.ds(start, LN_ROWS), :] = y[:, j * C:(j + 1) * C].astype(BF16)
+            base = pl.multiple_of((i % blocks) * LN_ROWS, LN_ROWS)
+            sums = dot(xbuf[t, pl.ds(base, LN_ROWS), :], ones)
+            for part in range(LN_ROWS // LN_PART):
+                start = pl.multiple_of(base + part * LN_PART, LN_PART)
+                x = xbuf[t, pl.ds(start, LN_PART), :].astype(F32)
+                mean = sums[part * LN_PART:(part + 1) * LN_PART] / DV
+                centred = x - jnp.concatenate([mean] * (DV // 128), axis=1)
+                variance = jnp.mean(centred * centred, axis=-1, keepdims=True)
+                y = centred * lax.rsqrt(variance + EPSILON) * gain_row
+                for j in range(F):
+                    normed[t, j, pl.ds(start, LN_PART), :] = y[:, j * C:(j + 1) * C].astype(BF16)
             return carry
         lax.fori_loop(lo_block, hi_block, body, 0)
 
-    cuts = (3 * T * blocks // 8, 5 * T * blocks // 8)
+    cuts = (T * blocks // 4, T * blocks // 2)
     for c in ld_x:
         c.wait()
     norm_blocks(0, cuts[0])
@@ -241,8 +251,16 @@
     ld_wo.wait()
     arrive(4, r4)
 
-    summed = dot(r4[...].reshape(R * HP, C), wv[...]).reshape(R, HP, VW)
-    pooled_part = jnp.sum(jnp.where(own_head, summed, 0.0), axis=1)
+    summed = dot(r4[...].reshape(R * HP, C), wv[...])
+    side = lax.broadcasted_iota(jnp.int32, (R, 2 * VHD), 1) < VHD
+    pieces = []
+    for c in range(VW // (2 * VHD)):
+        sumbuf[c] = summed[:, c * 2 * VHD:(c + 1) * 2 * VHD]
+        pieces.append(jnp.where(
+            side,
+            sumbuf[c, pl.ds(2 * c, R, stride=HP), :],
+            sumbuf[c, pl.ds(2 * c + 1, R, stride=HP), :]))
+    pooled_part = jnp.concatenate(pieces, axis=1)
     for j in range(F):
         s5[j, :, 0:PC] = pooled_part[:, j * PC:(j + 1) * PC]
     scatter(5, s5, r5)
@@ -368,7 +386,7 @@
             *fan(F, (2 * R, D // 2), BF16),
             *fan(S, (2 * R, D // 2), BF16),
             *pair((R, up(OC, 128)), F32),
-            V((N, HC), F32), V((F, N, OC), F32),
+            V((N, HC), F32), V((F, N, OC), F32), V((VW // (2 * VHD), R * HP, 2 * VHD), F32),
             pltpu.SemaphoreType.DMA((13 + T,)),
             pltpu.SemaphoreType.DMA((9, F)), pltpu.SemaphoreType.DMA((9, F)),
             pltpu.SemaphoreType.DMA((2, S)), pltpu.SemaphoreType.DMA((2, S)),

time: 36.2 us -> 36.1 us (level)
  no operation moved by 1% of the time
where the time goes in v6:
time: 36.1 us; the launch traced here: 36 us
  Pallas kernels  34.7 us (96%)
  between operations  0.66 us (2%)
  local copies, waits for them, and re-layouts  0.6 us (2%)
    pallas_call x1, Pallas kernels, local(): pl.pallas_call(functools.partial(kernel, F, S), out_shape=pltpu.VMEM((R,...  34.7 us

profile of v6, /device:TPU:0, one launch (start us, length us, event | category | flops | bytes accessed | tf_op | source)
XLA Modules:
  0.0 36.0 jit_solution(1165355528357166596)
XLA Ops:
  0.7 34.7 %shard_map.136 = bf16[8,192]{1,0:T(8,128)(2,1)S(1)} custom-call(bf16[2,256,1536]{2,1,0:T(8,128)(2,1)} %patches.1, f32[1536]{0:T(1024)} %vit_gain_hbm.1, bf16[384,768]{1,0:T(8,128)(2,1)} %w_query.1, bf16[384,768]{1,0:T(8,128)(2,1)} %w_key.1, bf16[384,768]{1,0:T(8,128)(2,1)} %w_value.1, bf16[192,1536]{1,0:T(8,128)(2,1)} %w_out.1, bf16[384,768]{1,0:T(8,128)(2,1)} %w_proj.1, ...), custom_call_target="tpu_custom_call" | custom-call | flops 305135616 | bytes 8388608 | tf_op jit(solution)/shard_map/pallas_call | solution.py:367
  35.4 0.6 %copy.16 = bf16[8,192]{1,0:T(8,128)(2,1)} copy(bf16[8,192]{1,0:T(8,128)(2,1)S(1)} %shard_map.136) | data formatting | bytes 6144

commit v7 on v6

--- a/solution.py
+++ b/solution.py
@@ -232,30 +232,35 @@
 
     spread_query = jnp.where(own_head, query[:, None, :], 0.0).reshape(R * HP, VW)
     folded = dot_t(spread_query.astype(BF16), wk[...]).astype(BF16)
-    s3[...] = folded.reshape(F, T * HP, C)
-    scatter(3, s3, r3)
+    folded = folded.reshape(F, T, HP, C)
+    for t in range(T):
+        s3[t] = folded[:, t]
+        scatter(9 + 2 * t, s3.at[t], r3.at[t])
     norm_blocks(cuts[1], T * blocks)
-    arrive(3, r3)
-
     for t in range(T):
-        by_token = dot_t(normed[t, 0], r3[0])
+        arrive(9 + 2 * t, r3.at[t])
+        by_token = dot_t(normed[t, 0], r3[t, 0])
         for j in range(1, F):
-            by_token = by_token + dot_t(normed[t, j], r3[j])
-        scores = jnp.transpose(by_token)[t * HP:(t + 1) * HP]
+            by_token = by_token + dot_t(normed[t, j], r3[t, j])
+        scores = jnp.transpose(by_token)
         lifted = jnp.exp(scores / math.sqrt(VHD))
         probs = (lifted / jnp.sum(lifted, axis=-1, keepdims=True)).astype(BF16)
         for j in range(F):
-            s4[j, pl.ds(t * HP, HP), :] = dot(probs, normed[t, j]).astype(BF16)
-    scatter(4, s4, r4)
+            s4[t, j] = dot(probs, normed[t, j]).astype(BF16)
+        scatter(10 + 2 * t, s4.at[t], r4.at[t])
     ld_wv.wait()
     ld_wo.wait()
-    arrive(4, r4)
-
-    summed = dot(r4[...].reshape(R * HP, C), wv[...])
+
+    for t in range(T):
+        arrive(10 + 2 * t, r4.at[t])
+        summed = dot(r4[t].reshape(F * HP, C), wv[...])
+        for c in range(VW // (2 * VHD)):
+            for j in range(F):
+                sumbuf[c, pl.ds((j * T + t) * HP, HP), :] = summed[
+                    j * HP:(j + 1) * HP, c * 2 * VHD:(c + 1) * 2 * VHD]
     side = lax.broadcasted_iota(jnp.int32, (R, 2 * VHD), 1) < VHD
     pieces = []
     for c in range(VW // (2 * VHD)):
-        sumbuf[c] = summed[:, c * 2 * VHD:(c + 1) * 2 * VHD]
         pieces.append(jnp.where(
             side,
             sumbuf[c, pl.ds(2 * c, R, stride=HP), :],
@@ -379,8 +384,7 @@
             *fan(F, (8, L), jnp.int32),
             *fan(S, (8, L), jnp.int32),
             *fan(F, (2 * R, VW // 2), BF16),
-            *pair((T * HP, C), BF16),
-            *pair((T * HP, C), BF16),
+            *[V((T, F, HP, C), BF16)] * 4,
             *pair((R, up(PC, 128)), F32),
             *pair((R, C), F32),
             *fan(F, (2 * R, D // 2), BF16),
@@ -388,7 +392,7 @@
             *pair((R, up(OC, 128)), F32),
             V((N, HC), F32), V((F, N, OC), F32), V((VW // (2 * VHD), R * HP, 2 * VHD), F32),
             pltpu.SemaphoreType.DMA((13 + T,)),
-            pltpu.SemaphoreType.DMA((9, F)), pltpu.SemaphoreType.DMA((9, F)),
+            *[pltpu.SemaphoreType.DMA((9 + 2 * T, F))] * 2,
             pltpu.SemaphoreType.DMA((2, S)), pltpu.SemaphoreType.DMA((2, S)),
         ],
         compiler_params=pltpu.CompilerParams(

time: 36.1 us -> 36.2 us (level)
  no operation moved by 1% of the time
where the time goes in v7:
time: 36.2 us; the launch traced here: 36.1 us
  Pallas kernels  34.8 us (96%)
  between operations  0.66 us (2%)
  local copies, waits for them, and re-layouts  0.6 us (2%)
    pallas_call x1, Pallas kernels, local(): pl.pallas_call(functools.partial(kernel, F, S), out_shape=pltpu.VMEM((R,...  34.8 us

profile of v7, /device:TPU:0, one launch (start us, length us, event | category | flops | bytes accessed | tf_op | source)
XLA Modules:
  0.0 36.1 jit_solution(17886904582965165424)
XLA Ops:
  0.7 34.8 %shard_map.136 = bf16[8,192]{1,0:T(8,128)(2,1)S(1)} custom-call(bf16[2,256,1536]{2,1,0:T(8,128)(2,1)} %patches.1, f32[1536]{0:T(1024)} %vit_gain_hbm.1, bf16[384,768]{1,0:T(8,128)(2,1)} %w_query.1, bf16[384,768]{1,0:T(8,128)(2,1)} %w_key.1, bf16[384,768]{1,0:T(8,128)(2,1)} %w_value.1, bf16[192,1536]{1,0:T(8,128)(2,1)} %w_out.1, bf16[384,768]{1,0:T(8,128)(2,1)} %w_proj.1, ...), custom_call_target="tpu_custom_call" | custom-call | flops 305135616 | bytes 8388608 | tf_op jit(solution)/shard_map/pallas_call | solution.py:372
  35.5 0.6 %copy.16 = bf16[8,192]{1,0:T(8,128)(2,1)} copy(bf16[8,192]{1,0:T(8,128)(2,1)S(1)} %shard_map.136) | data formatting | bytes 6144
